TPU v7x, 128 devices: a whole 4x4x4 slice. The times are simulated.
128 devices in a mesh: gx: 8 (over x_hi, y), gy: 16 (over z, x_lo, core).
Axes of the slice: x: 4 (x_hi: 2, x_lo: 2; x = x_hi * 2 + x_lo), y: 4, z: 4, core: 2. Of those that a mesh axis runs over, the one named last changes fastest.
Arguments:
- start_potentials: float32 [128, 256, 16, 128], P('gx', 'gy'), may hold values from -6 to 6
- conductivity: float32 [128, 256, 16], P('gx', 'gy'), may hold values from 0.2 to 5
- electrodes: int32 [128, 2], replicated, may hold values from 0 to 32767
- coarse_inverse: float32 [4096, 4096], P(('gx', 'gy')), as said below
Outputs:
- potentials: float32 [128, 256, 16, 128], P('gx', 'gy')
- residual: float32 [128, 256, 16, 128], P('gx', 'gy')
Inputs may be any that keep to these rules, and one draw needn't show every extreme that they name: electrodes[f, k] is the index x * 256 + y of a cell at depth 0. coarse_inverse is exactly symmetric.
All inputs are finite; a program needn't handle non-finite values.
Results may differ from a plain program's by a relative error of at most 0.0003.
Values sent between devices are 32-bit elements; how exact they have to be, the bound alone decides.
A program may use at most 128 MiB of HBM per device.

v0:
```python
import jax
import jax.numpy as jnp
from jax import lax
from jax.sharding import PartitionSpec as P

DELTA = 2
SWEEPS = 4
ITERS = 2
CSX = 4
CSY = 4
CSZ = 2


OMEGA = 0.7
CURRENT = 8.0


def extended(block, sides, width):
    for axis, dim in sides:
        count = lax.axis_size(axis)
        forward = [(i, i + 1) for i in range(count - 1)]
        backward = [(target, source) for source, target in forward]
        low = lax.ppermute(
            lax.slice_in_dim(block, block.shape[dim] - width, None, axis=dim), axis, forward
        )
        high = lax.ppermute(lax.slice_in_dim(block, 0, width, axis=dim), axis, backward)
        block = jnp.concatenate([low, block, high], axis=dim)
    return block


def face_terms(sigma_pad, inside):
    centre = sigma_pad[1:-1, 1:-1]
    layers = centre.shape[2]
    zero_layer = jnp.zeros(centre.shape[:2] + (1,), centre.dtype)
    deeper = jnp.concatenate([centre[:, :, 1:], zero_layer], axis=2)
    shallower = jnp.concatenate([zero_layer, centre[:, :, :-1]], axis=2)
    surface = (jnp.arange(layers) > 0).astype(centre.dtype)
    west_face = 0.5 * (centre + sigma_pad[:-2, 1:-1]) * inside
    east_face = 0.5 * (centre + sigma_pad[2:, 1:-1]) * inside
    south_face = 0.5 * (centre + sigma_pad[1:-1, :-2]) * inside
    north_face = 0.5 * (centre + sigma_pad[1:-1, 2:]) * inside
    lower_face = 0.5 * (centre + deeper) * inside
    upper_face = 0.5 * (centre + shallower) * inside * surface
    return (west_face, east_face, south_face, north_face, lower_face, upper_face)


def apply_op(couplings, padded):
    west_face, east_face, south_face, north_face, lower_face, upper_face = [
        c[..., None] for c in couplings
    ]
    values = padded[1:-1, 1:-1]
    zero_layer = jnp.zeros(values.shape[:2] + (1, values.shape[3]), values.dtype)
    deeper = jnp.concatenate([values[:, :, 1:], zero_layer], axis=2)
    shallower = jnp.concatenate([zero_layer, values[:, :, :-1]], axis=2)
    total_face = west_face + east_face + south_face + north_face + lower_face + upper_face
    beside = (
        west_face * padded[:-2, 1:-1]
        + east_face * padded[2:, 1:-1]
        + south_face * padded[1:-1, :-2]
        + north_face * padded[1:-1, 2:]
        + lower_face * deeper
        + upper_face * shallower
    )
    return total_face * values - beside


def local_solve(couplings, inside, residual_part):
    diagonal = (
        couplings[0]
        + couplings[1]
        + couplings[2]
        + couplings[3]
        + couplings[4]
        + couplings[5]
        + (1.0 - inside)
    )
    step_size = (OMEGA / diagonal)[..., None]
    estimate = step_size * residual_part
    for sweep_index in range(SWEEPS - 1):
        widened = jnp.pad(estimate, ((1, 1), (1, 1), (0, 0), (0, 0)))
        estimate = estimate + step_size * (residual_part - apply_op(couplings, widened))
    return estimate


def forcing_field(row_global, col_global, inside_plane, electrodes, grid_cols, layers):
    cell_index = row_global[:, None] * grid_cols + col_global[None, :]
    source_hit = (cell_index[:, :, None] == electrodes[None, None, :, 0]).astype(inside_plane.dtype)
    sink_hit = (cell_index[:, :, None] == electrodes[None, None, :, 1]).astype(inside_plane.dtype)
    surface_term = CURRENT * (source_hit - sink_hit) * inside_plane[:, :, None]
    below = jnp.zeros(
        surface_term.shape[:2] + (layers - 1, surface_term.shape[2]), surface_term.dtype
    )
    return jnp.concatenate([surface_term[:, :, None, :], below], axis=2)


def rim_single(values):
    return extended(values, (("gx", 0), ("gy", 1)), 1)


def widen(values):
    return extended(values, (("gx", 0), ("gy", 1)), DELTA)


def restrict(field_part):
    rows_dev, cols_dev, layers, fields = field_part.shape
    grouped = field_part.reshape(
        CSX, rows_dev // CSX, CSY, cols_dev // CSY, CSZ, layers // CSZ, fields
    )
    return jnp.sum(grouped, axis=(1, 3, 5)).reshape(CSX * CSY * CSZ, fields)


def prolong(coarse_corr, rows_dev, cols_dev, layers):
    fields = coarse_corr.shape[1]
    blocks = coarse_corr.reshape(CSX, CSY, CSZ, fields)
    spread = jnp.broadcast_to(
        blocks[:, None, :, None, :, None, :],
        (CSX, rows_dev // CSX, CSY, cols_dev // CSY, CSZ, layers // CSZ, fields),
    )
    return spread.reshape(rows_dev, cols_dev, layers, fields)


def coarse_solve(coarse_res, coarse_inverse):
    return jnp.dot(
        coarse_inverse,
        lax.all_gather(coarse_res, ("gx", "gy"), axis=0, tiled=True),
        precision=lax.Precision.HIGHEST,
        preferred_element_type=jnp.float32,
    )


def on_device(start_potentials, conductivity, electrodes, coarse_inverse):
    rows_dev, cols_dev, layers, fields = start_potentials.shape
    margin = DELTA
    grid_rows = rows_dev * lax.axis_size("gx")
    grid_cols = cols_dev * lax.axis_size("gy")
    row_anchor = lax.axis_index("gx") * rows_dev
    col_anchor = lax.axis_index("gy") * cols_dev
    sigma_wide = extended(conductivity, (("gx", 0), ("gy", 1)), DELTA + 1)
    row_global = row_anchor - margin + jnp.arange(rows_dev + 2 * margin, dtype=jnp.int32)
    col_global = col_anchor - margin + jnp.arange(cols_dev + 2 * margin, dtype=jnp.int32)
    row_inside = ((row_global >= 0) & (row_global < grid_rows)).astype(jnp.float32)
    col_inside = ((col_global >= 0) & (col_global < grid_cols)).astype(jnp.float32)
    inside_plane = row_inside[:, None] * col_inside[None, :]
    inside_wide = inside_plane[:, :, None] * jnp.ones((1, 1, layers), jnp.float32)
    couplings_wide = face_terms(sigma_wide, inside_wide)
    couplings_own = tuple(
        (
            coupling[margin : margin + rows_dev, margin : margin + cols_dev]
            for coupling in couplings_wide
        )
    )
    own_rows = row_anchor + jnp.arange(rows_dev, dtype=jnp.int32)
    own_cols = col_anchor + jnp.arange(cols_dev, dtype=jnp.int32)
    forcing_own = forcing_field(
        own_rows,
        own_cols,
        jnp.ones((rows_dev, cols_dev), jnp.float32),
        electrodes,
        grid_cols,
        layers,
    )
    residual_own = forcing_own - apply_op(couplings_own, rim_single(start_potentials))
    residual_wide = widen(residual_own)
    potentials = start_potentials
    for iteration in range(ITERS):
        fine = local_solve(couplings_wide, inside_wide, residual_wide)[
            margin : margin + rows_dev, margin : margin + cols_dev
        ]
        coarse_corr = coarse_solve(restrict(residual_own), coarse_inverse)
        correction = fine + prolong(coarse_corr, rows_dev, cols_dev, layers)
        potentials = potentials + correction
        residual_own = residual_own - apply_op(couplings_own, rim_single(correction))
        if iteration + 1 < ITERS:
            residual_wide = widen(residual_own)
    return (potentials, residual_own)


def solution(mesh):
    in_specs = (P("gx", "gy", None, None), P("gx", "gy", None), P(), P(("gx", "gy"), None))
    out_specs = (P("gx", "gy", None, None), P("gx", "gy", None, None))
    return jax.shard_map(
        on_device, mesh=mesh, in_specs=in_specs, out_specs=out_specs, check_vma=False
    )
```

profile of v0, /device:TPU:5, one launch (start us, length us, event | category | flops | bytes accessed | tf_op | source)
XLA Modules:
  0.0 597.9 jit_solution(12965383170208886)
XLA Ops:
  11.2 5.7 collective-permute-start.1
  21.2 7.0 %collective-permute-start.5 = (f32[1,16,16,128]{3,1,2,0:T(8,128)S(1)}, f32[1,16,16,128]{3,1,2,0:T(8,128)S(1)}, u32[]{:S(2)}, u32[]{:S(2)}) collective-permute-start(f32[1,16,16,128]{3,1,2,0:T(8,128)S(1)} %get-tuple-element.58), channel_id=1, source_target_pairs={{16,0},{32,16},{48,32},{64,48},{80,64},{96,80},{112,96},{17,1},{33... | collective-permute-start | bytes 393224 | tf_op jit(solution)/shard_map/ppermute | solution.py:26
  31.5 4.5 collective-permute-start.2
  37.9 3.4 collective-permute-done.3
  50.3 4.6 collective-permute-done.7
  55.6 7.1 %fusion.103 = f32[16,16,16,128]{3,1,2,0:T(8,128)S(1)} fusion(f32[18,1,16,128]{3,1,2,0:T(1,128)} %bitcast.43, f32[18,16,16,128]{3,1,2,0:T(8,128)} %copy-done.24, f32[18,1,16,128]{3,1,2,0:T(1,128)} %bitcast.42, f32[1,16,16,128]{3,1,2,0:T(8,128)} %copy-done.61, f32[16,16,16,128]{3,1,2,0:T(8,128)} %copy-done.8, f32[1,16,16,128]{3,1,2,0:T(8,128)} %copy-done.60, ...), kind=kLoop, calls=%fused_computation.154 | loop fusion | flops 9437184 | bytes 11288576 | tf_op jit(solution)/shard_map/sub | solution.py:162
  65.0 7.0 %collective-permute-start.9 = (f32[2,16,16,128]{3,1,2,0:T(8,128)S(1)}, f32[2,16,16,128]{3,1,2,0:T(8,128)S(1)}, u32[]{:S(2)}, u32[]{:S(2)}) collective-permute-start(f32[2,16,16,128]{3,1,2,0:T(8,128)S(1)} %get-tuple-element.55), channel_id=1, source_target_pairs={{16,0},{32,16},{48,32},{64,48},{80,64},{96,80},{112,96},{17,1},{33... | collective-permute-start | bytes 786440 | tf_op jit(solution)/shard_map/ppermute | solution.py:26
  76.3 4.1 collective-permute-start.10
  99.9 4.5 broadcast_multiply_fusion.1
  105.6 10.0 %fusion.9 = f32[20,20,16,128]{3,1,2,0:T(8,128)S(1)} fusion(f32[20,20,16,128]{3,1,2,0:T(8,128)S(1)} %get-tuple-element.32, f32[20,20,15,128]{3,1,2,0:T(8,128)S(1)} %get-tuple-element.29, f32[20,20,15,128]{3,1,2,0:T(8,128)S(1)} %get-tuple-element.28, f32[20,20,16]{1,2,0:T(8,128)S(1)} %copy-done.12, f32[20,20,16]{1,2,0:T(8,128)S(1)} %copy-done.10, ...), kind=kLoop, calls=%fused_computation.33 | loop fusion | flops 16384000 | bytes 16179200 | tf_op jit(solution)/shard_map/add | solution.py:81
  116.1 10.1 %fusion.22 = f32[20,20,16,128]{3,1,2,0:T(8,128)S(1)} fusion(f32[20,20,16,128]{3,1,2,0:T(8,128)S(1)} %fusion.9, f32[20,20,15,128]{3,1,2,0:T(8,128)S(1)} %get-tuple-element.27, f32[20,20,15,128]{3,1,2,0:T(8,128)S(1)} %get-tuple-element.26, f32[20,20,16]{1,2,0:T(8,128)S(1)} %copy-done.12, f32[20,20,16]{1,2,0:T(8,128)S(1)} %copy-done.10, ...), kind=kLoop, calls=%fused_computation.46 | loop fusion | flops 16384000 | bytes 16179200 | tf_op jit(solution)/shard_map/add | solution.py:81
  128.8 3.2 pad_multiply_fusion.1
  132.1 5.7 fusion.29
  137.8 158.1 %all-gather.3.cloned.1.call-done = f32[4096,128]{1,0:T(8,128)} async-done(((f32[32,128]{1,0:T(8,128)}), f32[4096,128]{1,0:T(8,128)}) %all-gather.3.cloned.1.call-update) | async-done | bytes 2097168 | tf_op jit(solution)/shard_map/all_gather | solution.py:125
  299.4 5.9 fusion.95
  307.9 6.3 %collective-permute-start.13 = (f32[1,16,16,128]{3,1,2,0:T(8,128)S(1)}, f32[1,16,16,128]{3,1,2,0:T(8,128)S(1)}, u32[]{:S(2)}, u32[]{:S(2)}) collective-permute-start(f32[1,16,16,128]{3,1,2,0:T(8,128)S(1)} %get-tuple-element.53), channel_id=1, source_target_pairs={{16,0},{32,16},{48,32},{64,48},{80,64},{96,80},{112,96},{17,1},{33... | collective-permute-start | bytes 393224 | tf_op jit(solution)/shard_map/ppermute | solution.py:26
  316.4 4.7 collective-permute-start.14
  323.6 4.2 collective-permute-done.15
  327.9 4.8 fusion.87
  334.7 7.1 %collective-permute-start.17 = (f32[2,16,16,128]{3,1,2,0:T(8,128)S(1)}, f32[2,16,16,128]{3,1,2,0:T(8,128)S(1)}, u32[]{:S(2)}, u32[]{:S(2)}) collective-permute-start(f32[2,16,16,128]{3,1,2,0:T(8,128)S(1)} %get-tuple-element.49), channel_id=1, source_target_pairs={{16,0},{32,16},{48,32},{64,48},{80,64},{96,80},{112,96},{17,1},{33... | collective-permute-start | bytes 786440 | tf_op jit(solution)/shard_map/ppermute | solution.py:26
  346.8 3.4 collective-permute-start.18
  355.7 6.1 %collective-permute-done.19 = f32[20,2,16,128]{3,2,1,0:T(8,128)} collective-permute-done((f32[20,2,16,128]{3,2,1,0:T(8,128)}, f32[20,2,16,128]{3,2,1,0:T(8,128)}, u32[]{:S(2)}, u32[]{:S(2)}) %collective-permute-start.19) | collective-permute-done | bytes 327712 | tf_op jit(solution)/shard_map/ppermute | solution.py:26
  362.9 4.5 pad_maximum_fusion.1
  368.7 10.0 %fusion.42 = f32[20,20,16,128]{3,1,2,0:T(8,128)S(1)} fusion(f32[20,20,16,128]{3,1,2,0:T(8,128)S(1)} %get-tuple-element.31, f32[20,20,15,128]{3,1,2,0:T(8,128)S(1)} %get-tuple-element.23, f32[20,20,15,128]{3,1,2,0:T(8,128)S(1)} %get-tuple-element.22, f32[20,20,16]{1,2,0:T(8,128)S(1)} %copy-done.13, f32[20,20,16]{1,2,0:T(8,128)S(1)} %copy-done.11, ...), kind=kLoop, calls=%fused_computation.66 | loop fusion | flops 16384000 | bytes 16179200 | tf_op jit(solution)/shard_map/add | solution.py:81
  379.2 10.1 %fusion.55 = f32[20,20,16,128]{3,1,2,0:T(8,128)S(1)} fusion(f32[20,20,16,128]{3,1,2,0:T(8,128)S(1)} %fusion.42, f32[20,20,15,128]{3,1,2,0:T(8,128)S(1)} %get-tuple-element.21, f32[20,20,15,128]{3,1,2,0:T(8,128)S(1)} %get-tuple-element.20, f32[20,20,16]{1,2,0:T(8,128)S(1)} %copy-done.13, f32[20,20,16]{1,2,0:T(8,128)S(1)} %copy-done.11, ...), kind=kLoop, calls=%fused_computation.79 | loop fusion | flops 16384000 | bytes 16179200 | tf_op jit(solution)/shard_map/add | solution.py:81
  391.9 3.2 pad_multiply_fusion
  395.1 5.7 fusion.62
  400.9 150.7 %all-gather.5.cloned.1.call-done = f32[4096,128]{1,0:T(8,128)} async-done(((f32[32,128]{1,0:T(8,128)}), f32[4096,128]{1,0:T(8,128)}) %all-gather.5.cloned.1.call-update) | async-done | bytes 2097168 | tf_op jit(solution)/shard_map/all_gather | solution.py:125
  555.0 7.0 %add_add_fusion = (f32[16,16,16,128]{3,1,2,0:T(8,128)S(1)}, f32[16,16,16,128]{3,1,2,0:T(8,128)S(1)}) fusion(f32[16,16,16,128]{3,1,2,0:T(8,128)} %copy-done.7, f32[16,16,16,128]{3,2,1,0:T(8,128)} %param.4, f32[16,16,16,128]{3,1,2,0:T(8,128)S(1)} %bitcast.34, f32[20,20,15,128]{3,1,2,0:T(8,128)} %get-tuple-element.19, f32[16,16,16]{1,2,0:T(8,128)S(1)} %copy-done.57, ...), kind=kLoop, calls=%fused_computation.163 | loop fusion | flops 5767168 | bytes 21995520 | tf_op jit(solution)/shard_map/add | solution.py:171
  564.6 6.3 %collective-permute-start.21 = (f32[1,16,16,128]{3,1,2,0:T(8,128)S(1)}, f32[1,16,16,128]{3,1,2,0:T(8,128)S(1)}, u32[]{:S(2)}, u32[]{:S(2)}) collective-permute-start(f32[1,16,16,128]{3,1,2,0:T(8,128)S(1)} %get-tuple-element.47), channel_id=1, source_target_pairs={{16,0},{32,16},{48,32},{64,48},{80,64},{96,80},{112,96},{17,1},{33... | collective-permute-start | bytes 393224 | tf_op jit(solution)/shard_map/ppermute | solution.py:26
  573.1 4.7 collective-permute-start.22
  584.3 4.8 fusion.71
  (246 shorter events, 98.1 us)
Async XLA Ops:
  7.2 288.8 %copy-start = (f32[32,4096]{1,0:T(8,128)S(1)}, f32[32,4096]{1,0:T(8,128)}, u32[]{:S(2)}) copy-start(f32[32,4096]{1,0:T(8,128)} %param.7) | copy-start | bytes 1572868
  7.2 288.7 %all-gather.3.cloned.1.call-start = ((), (), s32[]{:S(2)}) async-start(), calls=%async_computation | async-start | bytes 2113536 | tf_op jit(solution)/shard_map/all_gather | solution.py:125
  8.0 23.3 %collective-permute-start = (f32[3,16,16]{2,1,0:T(8,128)S(1)}, f32[3,16,16]{2,1,0:T(8,128)S(1)}, u32[]{:S(2)}, u32[]{:S(2)}) collective-permute-start(f32[3,16,16]{2,1,0:T(8,128)S(1)} %get-tuple-element.72), channel_id=1, source_target_pairs={{0,16},{16,32},{32,48},{48,64},{64,80},{80,96},{96,112},{1,17},{17... | collective-permute-start | bytes 9224 | tf_op jit(solution)/shard_map/ppermute | solution.py:23
  11.2 20.2 %collective-permute-start.1 = (f32[3,16,16]{2,1,0:T(8,128)S(1)}, f32[3,16,16]{2,1,0:T(8,128)S(1)}, u32[]{:S(2)}, u32[]{:S(2)}) collective-permute-start(f32[3,16,16]{2,1,0:T(8,128)S(1)} %get-tuple-element.71), channel_id=1, source_target_pairs={{16,0},{32,16},{48,32},{64,48},{80,64},{96,80},{112,96},{17,1},{33... | collective-permute-start | bytes 9224 | tf_op jit(solution)/shard_map/ppermute | solution.py:26
  19.2 23.4 %collective-permute-start.4 = (f32[1,16,16,128]{3,1,2,0:T(8,128)S(1)}, f32[1,16,16,128]{3,1,2,0:T(8,128)S(1)}, u32[]{:S(2)}, u32[]{:S(2)}) collective-permute-start(f32[1,16,16,128]{3,1,2,0:T(8,128)S(1)} %get-tuple-element.59), channel_id=1, source_target_pairs={{0,16},{16,32},{32,48},{48,64},{64,80},{80,96},{96,112},{1,17},{17... | collective-permute-start | bytes 393224 | tf_op jit(solution)/shard_map/ppermute | solution.py:23
  21.2 22.2 %collective-permute-start.5 = (f32[1,16,16,128]{3,1,2,0:T(8,128)S(1)}, f32[1,16,16,128]{3,1,2,0:T(8,128)S(1)}, u32[]{:S(2)}, u32[]{:S(2)}) collective-permute-start(f32[1,16,16,128]{3,1,2,0:T(8,128)S(1)} %get-tuple-element.58), channel_id=1, source_target_pairs={{16,0},{32,16},{48,32},{64,48},{80,64},{96,80},{112,96},{17,1},{33... | collective-permute-start | bytes 393224 | tf_op jit(solution)/shard_map/ppermute | solution.py:26
  31.5 6.5 %collective-permute-start.2 = (f32[22,3,16]{2,1,0:T(4,128)S(1)}, f32[22,3,16]{2,1,0:T(4,128)S(1)}, u32[]{:S(2)}, u32[]{:S(2)}) collective-permute-start(f32[22,3,16]{2,1,0:T(4,128)S(1)} %get-tuple-element.69), channel_id=1, source_target_pairs={{0,1},{1,2},{2,3},{3,4},{4,5},{5,6},{6,7},{7,8},{8,9},{9,10},{10,1... | collective-permute-start | bytes 12680 | tf_op jit(solution)/shard_map/ppermute | solution.py:23
  36.0 5.4 collective-permute-start.3
  45.1 5.3 collective-permute-start.6
  47.0 7.9 %collective-permute-start.7 = (f32[18,1,16,128]{3,2,1,0:T(8,128)S(1)}, f32[18,1,16,128]{3,2,1,0:T(8,128)S(1)}, u32[]{:S(2)}, u32[]{:S(2)}) collective-permute-start(f32[18,1,16,128]{3,2,1,0:T(8,128)S(1)} %bitcast.36), channel_id=1, source_target_pairs={{1,0},{2,1},{3,2},{4,3},{5,4},{6,5},{7,6},{8,7},{9,8},{10,9},{11,1... | collective-permute-start | bytes 442376 | tf_op jit(solution)/shard_map/ppermute | solution.py:26
  62.8 11.0 %collective-permute-start.8 = (f32[2,16,16,128]{3,1,2,0:T(8,128)S(1)}, f32[2,16,16,128]{3,1,2,0:T(8,128)S(1)}, u32[]{:S(2)}, u32[]{:S(2)}) collective-permute-start(f32[2,16,16,128]{3,1,2,0:T(8,128)S(1)} %get-tuple-element.54), channel_id=1, source_target_pairs={{0,16},{16,32},{32,48},{48,64},{64,80},{80,96},{96,112},{1,17},{17... | collective-permute-start | bytes 786440 | tf_op jit(solution)/shard_map/ppermute | solution.py:23
  65.0 10.3 %collective-permute-start.9 = (f32[2,16,16,128]{3,1,2,0:T(8,128)S(1)}, f32[2,16,16,128]{3,1,2,0:T(8,128)S(1)}, u32[]{:S(2)}, u32[]{:S(2)}) collective-permute-start(f32[2,16,16,128]{3,1,2,0:T(8,128)S(1)} %get-tuple-element.55), channel_id=1, source_target_pairs={{16,0},{32,16},{48,32},{64,48},{80,64},{96,80},{112,96},{17,1},{33... | collective-permute-start | bytes 786440 | tf_op jit(solution)/shard_map/ppermute | solution.py:26
  76.3 21.3 %collective-permute-start.10 = (f32[20,2,16,128]{3,2,1,0:T(8,128)}, f32[20,2,16,128]{3,2,1,0:T(8,128)}, u32[]{:S(2)}, u32[]{:S(2)}) collective-permute-start(f32[20,2,16,128]{3,2,1,0:T(8,128)} %copy.102), channel_id=1, source_target_pairs={{0,1},{1,2},{2,3},{3,4},{4,5},{5,6},{6,7},{7,8},{8,9},{9,10},{10,1... | collective-permute-start | bytes 983048 | tf_op jit(solution)/shard_map/ppermute | solution.py:23
  81.1 17.6 %collective-permute-start.11 = (f32[20,2,16,128]{3,2,1,0:T(8,128)}, f32[20,2,16,128]{3,2,1,0:T(8,128)}, u32[]{:S(2)}, u32[]{:S(2)}) collective-permute-start(f32[20,2,16,128]{3,2,1,0:T(8,128)} %copy.103), channel_id=1, source_target_pairs={{1,0},{2,1},{3,2},{4,3},{5,4},{6,5},{7,6},{8,7},{9,8},{10,9},{11,1... | collective-permute-start | bytes 983048 | tf_op jit(solution)/shard_map/ppermute | solution.py:26
  97.3 454.2 %all-gather.5.cloned.1.call-start = ((), (), s32[]{:S(2)}) async-start(), calls=%async_computation.1 | async-start | bytes 2113536 | tf_op jit(solution)/shard_map/all_gather | solution.py:125
  137.8 161.5 %copy-start.54 = (f32[16,16,16]{1,2,0:T(8,128)S(1)}, f32[16,16,16]{1,2,0:T(8,128)}, u32[]{:S(2)}) copy-start(f32[16,16,16]{1,2,0:T(8,128)} %slice.435) | copy-start | bytes 49156
  137.8 161.5 %copy-start.56 = (f32[16,16,16]{1,2,0:T(8,128)S(1)}, f32[16,16,16]{1,2,0:T(8,128)}, u32[]{:S(2)}) copy-start(f32[16,16,16]{1,2,0:T(8,128)} %slice.431) | copy-start | bytes 49156
  137.8 161.5 %copy-start.58 = (f32[16,16,16]{1,2,0:T(8,128)S(1)}, f32[16,16,16]{1,2,0:T(8,128)}, u32[]{:S(2)}) copy-start(f32[16,16,16]{1,2,0:T(8,128)} %slice.432) | copy-start | bytes 49156
  305.3 9.3 %collective-permute-start.12 = (f32[1,16,16,128]{3,1,2,0:T(8,128)S(1)}, f32[1,16,16,128]{3,1,2,0:T(8,128)S(1)}, u32[]{:S(2)}, u32[]{:S(2)}) collective-permute-start(f32[1,16,16,128]{3,1,2,0:T(8,128)S(1)} %get-tuple-element.52), channel_id=1, source_target_pairs={{0,16},{16,32},{32,48},{48,64},{64,80},{80,96},{96,112},{1,17},{17... | collective-permute-start | bytes 393224 | tf_op jit(solution)/shard_map/ppermute | solution.py:23
  307.9 8.3 %collective-permute-start.13 = (f32[1,16,16,128]{3,1,2,0:T(8,128)S(1)}, f32[1,16,16,128]{3,1,2,0:T(8,128)S(1)}, u32[]{:S(2)}, u32[]{:S(2)}) collective-permute-start(f32[1,16,16,128]{3,1,2,0:T(8,128)S(1)} %get-tuple-element.53), channel_id=1, source_target_pairs={{16,0},{32,16},{48,32},{64,48},{80,64},{96,80},{112,96},{17,1},{33... | collective-permute-start | bytes 393224 | tf_op jit(solution)/shard_map/ppermute | solution.py:26
  316.4 7.3 %collective-permute-start.14 = (f32[18,1,16,128]{3,2,1,0:T(8,128)S(1)}, f32[18,1,16,128]{3,2,1,0:T(8,128)S(1)}, u32[]{:S(2)}, u32[]{:S(2)}) collective-permute-start(f32[18,1,16,128]{3,2,1,0:T(8,128)S(1)} %bitcast.41), channel_id=1, source_target_pairs={{0,1},{1,2},{2,3},{3,4},{4,5},{5,6},{6,7},{7,8},{8,9},{9,10},{10,1... | collective-permute-start | bytes 442376 | tf_op jit(solution)/shard_map/ppermute | solution.py:23
  321.1 6.7 %collective-permute-start.15 = (f32[18,1,16,128]{3,2,1,0:T(8,128)S(1)}, f32[18,1,16,128]{3,2,1,0:T(8,128)S(1)}, u32[]{:S(2)}, u32[]{:S(2)}) collective-permute-start(f32[18,1,16,128]{3,2,1,0:T(8,128)S(1)} %bitcast.39), channel_id=1, source_target_pairs={{1,0},{2,1},{3,2},{4,3},{5,4},{6,5},{7,6},{8,7},{9,8},{10,9},{11,1... | collective-permute-start | bytes 442376 | tf_op jit(solution)/shard_map/ppermute | solution.py:26
  332.8 10.8 %collective-permute-start.16 = (f32[2,16,16,128]{3,1,2,0:T(8,128)S(1)}, f32[2,16,16,128]{3,1,2,0:T(8,128)S(1)}, u32[]{:S(2)}, u32[]{:S(2)}) collective-permute-start(f32[2,16,16,128]{3,1,2,0:T(8,128)S(1)} %get-tuple-element.48), channel_id=1, source_target_pairs={{0,16},{16,32},{32,48},{48,64},{64,80},{80,96},{96,112},{1,17},{17... | collective-permute-start | bytes 786440 | tf_op jit(solution)/shard_map/ppermute | solution.py:23
  334.7 10.6 %collective-permute-start.17 = (f32[2,16,16,128]{3,1,2,0:T(8,128)S(1)}, f32[2,16,16,128]{3,1,2,0:T(8,128)S(1)}, u32[]{:S(2)}, u32[]{:S(2)}) collective-permute-start(f32[2,16,16,128]{3,1,2,0:T(8,128)S(1)} %get-tuple-element.49), channel_id=1, source_target_pairs={{16,0},{32,16},{48,32},{64,48},{80,64},{96,80},{112,96},{17,1},{33... | collective-permute-start | bytes 786440 | tf_op jit(solution)/shard_map/ppermute | solution.py:26
  346.8 7.7 %collective-permute-start.18 = (f32[20,2,16,128]{3,2,1,0:T(8,128)}, f32[20,2,16,128]{3,2,1,0:T(8,128)}, u32[]{:S(2)}, u32[]{:S(2)}) collective-permute-start(f32[20,2,16,128]{3,2,1,0:T(8,128)} %copy.120), channel_id=1, source_target_pairs={{0,1},{1,2},{2,3},{3,4},{4,5},{5,6},{6,7},{7,8},{8,9},{9,10},{10,1... | collective-permute-start | bytes 983048 | tf_op jit(solution)/shard_map/ppermute | solution.py:23
  351.0 10.8 %collective-permute-start.19 = (f32[20,2,16,128]{3,2,1,0:T(8,128)}, f32[20,2,16,128]{3,2,1,0:T(8,128)}, u32[]{:S(2)}, u32[]{:S(2)}) collective-permute-start(f32[20,2,16,128]{3,2,1,0:T(8,128)} %copy.121), channel_id=1, source_target_pairs={{1,0},{2,1},{3,2},{4,3},{5,4},{6,5},{7,6},{8,7},{9,8},{10,9},{11,1... | collective-permute-start | bytes 983048 | tf_op jit(solution)/shard_map/ppermute | solution.py:26
  400.9 154.1 %copy-start.57 = (f32[16,16,16]{1,2,0:T(8,128)S(1)}, f32[16,16,16]{1,2,0:T(8,128)}, u32[]{:S(2)}) copy-start(f32[16,16,16]{1,2,0:T(8,128)} %slice.431) | copy-start | bytes 49156
  400.9 154.1 %copy-start.59 = (f32[16,16,16]{1,2,0:T(8,128)S(1)}, f32[16,16,16]{1,2,0:T(8,128)}, u32[]{:S(2)}) copy-start(f32[16,16,16]{1,2,0:T(8,128)} %slice.432) | copy-start | bytes 49156
  562.1 9.3 %collective-permute-start.20 = (f32[1,16,16,128]{3,1,2,0:T(8,128)S(1)}, f32[1,16,16,128]{3,1,2,0:T(8,128)S(1)}, u32[]{:S(2)}, u32[]{:S(2)}) collective-permute-start(f32[1,16,16,128]{3,1,2,0:T(8,128)S(1)} %get-tuple-element.46), channel_id=1, source_target_pairs={{0,16},{16,32},{32,48},{48,64},{64,80},{80,96},{96,112},{1,17},{17... | collective-permute-start | bytes 393224 | tf_op jit(solution)/shard_map/ppermute | solution.py:23
  564.6 8.3 %collective-permute-start.21 = (f32[1,16,16,128]{3,1,2,0:T(8,128)S(1)}, f32[1,16,16,128]{3,1,2,0:T(8,128)S(1)}, u32[]{:S(2)}, u32[]{:S(2)}) collective-permute-start(f32[1,16,16,128]{3,1,2,0:T(8,128)S(1)} %get-tuple-element.47), channel_id=1, source_target_pairs={{16,0},{32,16},{48,32},{64,48},{80,64},{96,80},{112,96},{17,1},{33... | collective-permute-start | bytes 393224 | tf_op jit(solution)/shard_map/ppermute | solution.py:26
  573.1 9.0 %collective-permute-start.22 = (f32[18,1,16,128]{3,2,1,0:T(8,128)S(1)}, f32[18,1,16,128]{3,2,1,0:T(8,128)S(1)}, u32[]{:S(2)}, u32[]{:S(2)}) collective-permute-start(f32[18,1,16,128]{3,2,1,0:T(8,128)S(1)} %bitcast.40), channel_id=1, source_target_pairs={{0,1},{1,2},{2,3},{3,4},{4,5},{5,6},{6,7},{7,8},{8,9},{9,10},{10,1... | collective-permute-start | bytes 442376 | tf_op jit(solution)/shard_map/ppermute | solution.py:23
  577.8 6.5 %collective-permute-start.23 = (f32[18,1,16,128]{3,2,1,0:T(8,128)S(1)}, f32[18,1,16,128]{3,2,1,0:T(8,128)S(1)}, u32[]{:S(2)}, u32[]{:S(2)}) collective-permute-start(f32[18,1,16,128]{3,2,1,0:T(8,128)S(1)} %bitcast.38), channel_id=1, source_target_pairs={{1,0},{2,1},{3,2},{4,3},{5,4},{6,5},{7,6},{8,7},{9,8},{10,9},{11,1... | collective-permute-start | bytes 442376 | tf_op jit(solution)/shard_map/ppermute | solution.py:26
  (60 other events, 579.7 us)
Sparse Core Ops, SparseCore 0:
  97.4 198.4 all-gather.2
  354.2 197.2 all-gather.4
where the time goes:
time: 604 us; the launch traced here: 598 us
  waiting for transfers between devices  340 us (56%)
  other arithmetic  100 us (17%)
  starting transfers between devices  89.8 us (15%)
  local copies, waits for them, and re-layouts  45.9 us (8%)
  between operations  15.4 us (3%)
  matrix products  6.06 us (1%)
    all_gather x2, waiting for transfers between devices, coarse_solve(): lax.all_gather(coarse_res, ('gx', 'gy'), axis=0, tiled=True)  309 us
    ppermute x12, starting transfers between devices, extended(): lax.ppermute(lax.slice_in_dim(block, 0, width, axis=dim), axis, backward)  51.9 us
    add x4, other arithmetic, local_solve(): estimate + step_size * (residual_part - apply_op(couplings, widened))  40.1 us
    ppermute x12, starting transfers between devices, extended(): lax.ppermute(lax.slice_in_dim(block, block.shape[dim] - width, None, axis...  37.7 us
    ppermute x12, waiting for transfers between devices, extended(): lax.ppermute(lax.slice_in_dim(block, 0, width, axis=dim), axis, backward)  26.7 us
  transfers between devices with their start and end apart: 26, of which 16 were waited for; matrix products, arithmetic and copies ran while one was open for 18% of the time, Pallas kernels for 0%

commit v1 on v0

v1 whole, which is shorter than its diff:
```python
import jax
import jax.numpy as jnp
from jax import lax
from jax.experimental import pallas as pl
from jax.experimental.pallas import tpu as pltpu
from jax.sharding import PartitionSpec as P

OMEGA = 0.7
CURRENT = 8.0
ITERS = 2
NI, NJ = 8, 16
B = 16
F = 128
E2 = B + 4
BLK = 32
MESH = pl.DeviceIdType.MESH
F32 = jnp.float32

SIDES = ((-1, 0), (1, 0), (0, -1), (0, 1))
CORNERS = ((-1, -1), (-1, 1), (1, -1), (1, 1))
AROUND = SIDES + CORNERS


def stencil(e, kx, ky, kz, x, y, p, memo):
    total = kx(x, y, p) * e(x - 1, y, p) + kx(x + 1, y, p) * e(x + 1, y, p)
    total = total + (ky(x, y, p) * e(x, y - 1, p) + ky(x, y + 1, p) * e(x, y + 1, p))
    other = e(x, y, 1 - p)
    if p == 0:
        across = pltpu.roll(kz(x, y, 1) * other, 1, 0)
    else:
        across = kz(x, y, 1) * pltpu.roll(other, 7, 0)
    return total + (kz(x, y, 0) * other + across)


def reader(ref, x0, y0, dx, dy):
    held = {}

    def get(x, y, p):
        key = (x, y, p)
        if key not in held:
            held[key] = ref[x0 + (x + dx), y0 + (y + dy), p]
        return held[key]

    return get


def blocks(x_lo, x_n, y_lo, y_n, xb, yb, body):
    def outer(n, carry):
        ix = n // (y_n // yb)
        iy = n % (y_n // yb)
        body(x_lo + ix * xb, y_lo + iy * yb)
        return carry

    lax.fori_loop(0, (x_n // xb) * (y_n // yb), outer, 0)


def kernel(
    v_hbm, cond_ref, elec_ref, cinv_hbm,
    pot_hbm, res_hbm,
    sig, sig_t, sig_b, v_nat, v_per, rr, bb, e_a, e_b, cc, kx, ky, kz, st, dg, res_nat,
    cblk, crow, gath, part, recv, pro, acc,
    sig_s, sig_r, v_s, v_r, c_s, c_r, ag_s, ag_r, rs_s, rs_r, r_s, r_r, h_s, h_r, loc,
):
    i = lax.axis_index("gx")
    j = lax.axis_index("gy")

    def there(dx, dy):
        ok = None
        for d, pos, n in ((dx, i, NI), (dy, j, NJ)):
            if d:
                term = (pos > 0) if d < 0 else (pos < n - 1)
                ok = term if ok is None else ok & term
        return ok

    own_v = pltpu.make_async_copy(v_hbm, v_nat.at[pl.ds(1, B), pl.ds(1, B)], loc.at[0])
    own_v.start()
    own_c = pltpu.make_async_copy(
        cinv_hbm.at[:, pl.ds(i * 512, 512)], cblk.at[pl.ds(i * BLK, BLK)], loc.at[1]
    )
    own_c.start()
    own_s = pltpu.make_async_copy(cond_ref, sig.at[pl.ds(3, B), pl.ds(8, B)], loc.at[2])
    own_s.start()

    bar = pltpu.get_barrier_semaphore()

    def greet_j(k, carry):
        pl.semaphore_signal(bar, inc=1, device_id=(i, lax.rem(j + k, NJ)), device_id_type=MESH)
        return carry

    lax.fori_loop(1, NJ, greet_j, 0)

    def greet_i(k, carry):
        pl.semaphore_signal(bar, inc=1, device_id=(lax.rem(i + k, NI), j), device_id_type=MESH)
        return carry

    lax.fori_loop(1, NI, greet_i, 0)
    count = jnp.int32(NJ - 1 + NI - 1)
    for dx, dy in CORNERS:
        ok = there(dx, dy)

        @pl.when(ok)
        def _():
            pl.semaphore_signal(bar, inc=1, device_id=(i + dx, j + dy), device_id_type=MESH)

        count = count + jnp.where(ok, 1, 0)
    pl.semaphore_wait(bar, count)

    def halo(dirs, make, what):
        for n, (dx, dy) in enumerate(dirs):
            if what in ("start", "sent"):

                @pl.when(there(dx, dy))
                def _():
                    copy = make(n, dx, dy)
                    copy.start() if what == "start" else copy.wait_send()

            else:

                @pl.when(there(-dx, -dy))
                def _():
                    make(n, dx, dy).wait_recv()

    def sig_copy(n, dx, dy):
        xs = {-1: (3, 3, 19), 0: (3, 16, 3), 1: (16, 3, 0)}[dx]
        ys = {-1: (8, 8, 24), 0: (8, 16, 8), 1: (16, 8, 0)}[dy]
        src = cond_ref.at[pl.ds(xs[0] - 3, xs[1]), pl.ds(ys[0] - 8, ys[1])]
        dst = sig.at[pl.ds(xs[2], xs[1]), pl.ds(ys[2], ys[1])]
        return pltpu.make_async_remote_copy(
            src_ref=src, dst_ref=dst, send_sem=sig_s.at[n], recv_sem=sig_r.at[n],
            device_id=(i + dx, j + dy), device_id_type=MESH)

    def edge(d, width, margin):
        return {
            -1: (margin, width, margin + B),
            0: (margin, B, margin),
            1: (margin + B - width, width, margin - width),
        }[d]

    def v_copy(n, dx, dy):
        xs, ys = edge(dx, 1, 1), edge(dy, 1, 1)
        return pltpu.make_async_remote_copy(
            src_ref=v_hbm.at[pl.ds(xs[0] - 1, xs[1]), pl.ds(ys[0] - 1, ys[1])],
            dst_ref=v_nat.at[pl.ds(xs[2], xs[1]), pl.ds(ys[2], ys[1])],
            send_sem=v_s.at[n], recv_sem=v_r.at[n],
            device_id=(i + dx, j + dy), device_id_type=MESH)

    def r_copy(it):
        def make(n, dx, dy):
            xs, ys = edge(dx, 2, 2), edge(dy, 2, 2)
            return pltpu.make_async_remote_copy(
                src_ref=rr.at[it, pl.ds(xs[0], xs[1]), pl.ds(ys[0], ys[1])],
                dst_ref=rr.at[it, pl.ds(xs[2], xs[1]), pl.ds(ys[2], ys[1])],
                send_sem=r_s.at[it, n], recv_sem=r_r.at[it, n],
                device_id=(i + dx, j + dy), device_id_type=MESH)
        return make

    def h_copy(it):
        def make(n, dx, dy):
            xs, ys = edge(dx, 1, 1), edge(dy, 1, 1)
            return pltpu.make_async_remote_copy(
                src_ref=cc.at[it, pl.ds(xs[0], xs[1]), pl.ds(ys[0], ys[1])],
                dst_ref=cc.at[it, pl.ds(xs[2], xs[1]), pl.ds(ys[2], ys[1])],
                send_sem=h_s.at[it, n], recv_sem=h_r.at[it, n],
                device_id=(i + dx, j + dy), device_id_type=MESH)
        return make

    halo(AROUND, sig_copy, "start")
    halo(SIDES, v_copy, "start")

    def c_copy(k, source):
        to = lax.rem(i + k, NI)
        return pltpu.make_async_remote_copy(
            src_ref=cinv_hbm.at[:, pl.ds(to * 512, 512)],
            dst_ref=cblk.at[pl.ds(source * BLK, BLK)],
            send_sem=c_s.at[k], recv_sem=c_r.at[k],
            device_id=(to, j), device_id_type=MESH)

    def c_start(k, carry):
        c_copy(k, i).start()
        return carry

    lax.fori_loop(1, NI, c_start, 0)

    def ag_copy(it, k, source):
        return pltpu.make_async_remote_copy(
            src_ref=crow.at[it],
            dst_ref=gath.at[it, pl.ds(source * BLK, BLK)],
            send_sem=ag_s.at[it, k], recv_sem=ag_r.at[it, k],
            device_id=(i, lax.rem(j + k, NJ)), device_id_type=MESH)

    def rs_copy(it, k, source):
        to = lax.rem(i + k, NI)
        return pltpu.make_async_remote_copy(
            src_ref=part.at[it, pl.ds(to * BLK, BLK)],
            dst_ref=recv.at[it, source],
            send_sem=rs_s.at[it, k], recv_sem=rs_r.at[it, k],
            device_id=(to, j), device_id_type=MESH)

    for dx, dy in AROUND:
        edge_here = ~there(dx, dy)

        @pl.when(edge_here)
        def _():
            xs = {-1: (0, 3), 0: (3, 16), 1: (19, 3)}[dx]
            ys = {-1: (0, 8), 0: (8, 16), 1: (24, 8)}[dy]
            sig[pl.ds(*xs), pl.ds(*ys)] = jnp.zeros((xs[1], ys[1], 16), F32)
            for it in range(ITERS):
                xr = {-1: (0, 2), 0: (2, B), 1: (B + 2, 2)}[dx]
                yr = {-1: (0, 2), 0: (2, B), 1: (B + 2, 2)}[dy]

                def zero_r(n, carry):
                    rr[it, xr[0] + n // yr[1], yr[0] + n % yr[1]] = jnp.zeros((2, 8, F), F32)
                    return carry

                lax.fori_loop(0, xr[1] * yr[1], zero_r, 0)
            if dx == 0 or dy == 0:
                xr = {-1: 0, 0: 1, 1: B + 1}[dx]
                yr = {-1: 0, 0: 1, 1: B + 1}[dy]

                def zero_v(n, carry):
                    at = (xr if dx else xr + n, yr if dy else yr + n)
                    v_nat[at[0], at[1]] = jnp.zeros((16, F), F32)
                    for it in range(ITERS):
                        cc[it, at[0], at[1]] = jnp.zeros((2, 8, F), F32)
                    return carry

                lax.fori_loop(0, B, zero_v, 0)

    def zero_ring(n, carry):
        zero = jnp.zeros((2, 8, F), F32)
        bb[0, n] = zero
        bb[E2 + 1, n] = zero
        bb[n, 0] = zero
        bb[n, E2 + 1] = zero
        return carry

    lax.fori_loop(0, E2 + 2, zero_ring, 0)

    def zero_ya(n, carry):
        zero = jnp.zeros((2, 8, F), F32)
        e_a[n, 0] = zero
        e_a[n, E2 + 1] = zero
        return carry

    def zero_faces(n, carry):
        zero = jnp.zeros((2, 8, F), F32)
        kx[E2, n] = zero
        ky[n, E2] = zero
        return carry

    lax.fori_loop(0, E2, zero_faces, 0)

    lax.fori_loop(0, E2 + 2, zero_ya, 0)

    own_s.wait()
    halo(AROUND, sig_copy, "here")

    def spread(x, carry):
        sig_t[...] = jnp.transpose(sig[x])
        for p in range(2):
            rows = sig_t[pl.ds(p, 8, stride=2), :]
            for y in range(E2 + 2):
                sig_b[x, y, p] = jnp.broadcast_to(rows[:, y + 5 : y + 6], (8, F))
        return carry

    lax.fori_loop(0, E2 + 2, spread, 0)

    level = lax.broadcasted_iota(jnp.int32, (8, F), 0)

    def faces(x0, y0):
        s = reader(sig_b, x0, y0, 1, 1)
        for x in range(2):
            for y in range(4):
                at = (x0 + x, y0 + y)
                even, odd = s(x, y, 0), s(x, y, 1)
                kz_in = 0.5 * (even + odd)
                next_even = jnp.where(level < 7, pltpu.roll(even, 7, 0), 0.0)
                bottom = 0.5 * (odd + next_even)
                kz_out = jnp.where(level < 7, bottom, 0.0)
                kz[at[0], at[1], 0] = kz_in
                kz[at[0], at[1], 1] = kz_out
                above = pltpu.roll(kz_out, 1, 0)
                for p in range(2):
                    west = 0.5 * (s(x, y, p) + s(x - 1, y, p))
                    east = 0.5 * (s(x, y, p) + s(x + 1, y, p))
                    south = 0.5 * (s(x, y, p) + s(x, y - 1, p))
                    north = 0.5 * (s(x, y, p) + s(x, y + 1, p))
                    depth = (kz_in + above) if p == 0 else (kz_in + bottom)
                    d = west + east + south + north + depth
                    kx[at[0], at[1], p] = west
                    ky[at[0], at[1], p] = south
                    dg[at[0], at[1], p] = d
                    st[at[0], at[1], p] = jnp.where(s(x, y, p) > 0.0, OMEGA / jnp.maximum(d, 1e-30), 0.0)

    blocks(0, E2, 0, E2, 2, 4, faces)

    own_v.wait()

    def permute(x, y):
        for p in range(2):
            v_per[x, y, p] = v_nat[x, y, pl.ds(p, 8, stride=2), :]

    def permute_own(n, carry):
        for y in range(B):
            permute(1 + n, 1 + y)
        return carry

    lax.fori_loop(0, B, permute_own, 0)
    halo(SIDES, v_copy, "here")

    def permute_rim(n, carry):
        permute(0, 1 + n)
        permute(B + 1, 1 + n)
        permute(1 + n, 0)
        permute(1 + n, B + 1)
        return carry

    lax.fori_loop(0, B, permute_rim, 0)

    cell = (i * B) * (NJ * B) + j * B
    source = elec_ref[0:1, :]
    sink = elec_ref[1:2, :]

    def first_residual(x0, y0):
        e = reader(v_per, x0, y0, 1, 1)
        fx, fy, fz = (reader(k, x0, y0, 2, 2) for k in (kx, ky, kz))
        for x in range(2):
            for y in range(4):
                here = cell + (x0 + x) * (NJ * B) + (y0 + y)
                force = jnp.where(source == here, CURRENT, 0.0) - jnp.where(sink == here, CURRENT, 0.0)
                force = jnp.where(level == 0, jnp.broadcast_to(force, (8, F)), 0.0)
                for p in range(2):
                    flow = stencil(e, fx, fy, fz, x, y, p, None) - dg[x0 + x + 2, y0 + y + 2, p] * e(x, y, p)
                    rr[0, x0 + x + 2, y0 + y + 2, p] = flow + force if p == 0 else flow

    blocks(0, B, 0, B, 2, 4, first_residual)

    for it in range(ITERS):
        halo(AROUND, r_copy(it), "start")

        def restrict(n, carry):
            a, b = n // 4, n % 4

            def add(x, total):
                for y in range(4):
                    for p in range(2):
                        total = total + rr[it, 2 + 4 * a + x, 2 + 4 * b + y, p]
                return total

            acc[pl.ds(pl.multiple_of(n * 8, 8), 8), :] = lax.fori_loop(0, 4, add, jnp.zeros((8, F), F32))
            return carry

        lax.fori_loop(0, 16, restrict, 0)
        rows = acc[pl.ds(0, BLK, stride=4), :]
        for q in range(1, 4):
            rows = rows + acc[pl.ds(q, BLK, stride=4), :]
        crow[it] = rows
        gath[it, pl.ds(pl.multiple_of(j * BLK, BLK), BLK)] = rows

        def ag_start(k, carry):
            ag_copy(it, k, j).start()
            return carry

        lax.fori_loop(1, NJ, ag_start, 0)

        if it == 0:
            own_c.wait()

            def c_wait(k, carry):
                c_copy(k, lax.rem(i - k + NI, NI)).wait_recv()
                return carry

            lax.fori_loop(1, NI, c_wait, 0)

        def ag_wait(k, carry):
            ag_copy(it, k, lax.rem(j - k + NJ, NJ)).wait_recv()
            return carry

        lax.fori_loop(1, NJ, ag_wait, 0)
        part[it] = jnp.dot(
            cblk[...], gath[it], precision=lax.Precision.HIGHEST, preferred_element_type=F32
        )

        def rs_start(k, carry):
            rs_copy(it, k, i).start()
            return carry

        lax.fori_loop(1, NI, rs_start, 0)

        halo(AROUND, r_copy(it), "here")

        def first_sweep(x0, y0):
            for x in range(2):
                for y in range(4):
                    for p in range(2):
                        bb[x0 + x + 1, y0 + y + 1, p] = st[x0 + x, y0 + y, p] * rr[it, x0 + x, y0 + y, p]

        blocks(0, E2, 0, E2, 2, 4, first_sweep)

        def sweep(src, store):
            def body(x0, y0):
                e = reader(src, x0, y0, 1, 1)
                fx, fy, fz = (reader(k, x0, y0, 0, 0) for k in (kx, ky, kz))
                for x in range(2):
                    for y in range(4):
                        for p in range(2):
                            nearby = stencil(e, fx, fy, fz, x, y, p, None)
                            value = ((1.0 - OMEGA) * e(x, y, p) + bb[x0 + x + 1, y0 + y + 1, p]
                                     + st[x0 + x, y0 + y, p] * nearby)
                            store(x0 + x, y0 + y, p, value)
            return body

        def into_a(x, y, p, value):
            e_a[x + 1, y + 1, p] = value

        def into_b(x, y, p, value):
            e_b[x + 1, y + 1, p] = value

        blocks(0, E2, 0, E2, 2, 4, sweep(bb, into_a))
        blocks(1, B + 2, 0, E2, 2, 4, sweep(e_a, into_b))

        def rs_wait(k, carry):
            rs_copy(it, k, lax.rem(i - k + NI, NI)).wait_recv()
            return carry

        lax.fori_loop(1, NI, rs_wait, 0)
        recv[it, i] = part[it, pl.ds(pl.multiple_of(i * BLK, BLK), BLK)]
        total = recv[it, 0]
        for q in range(1, NI):
            total = total + recv[it, q]
        for q in range(4):
            pro[pl.ds(q, BLK, stride=4), :] = total

        def correct(x0, y0):
            e = reader(e_b, x0, y0, 1, 1)
            fx, fy, fz = (reader(k, x0, y0, 0, 0) for k in (kx, ky, kz))
            block = ((x0 - 2) // 4) * 4 + (y0 - 2) // 4
            coarse = pro[pl.ds(pl.multiple_of(block * 8, 8), 8), :]
            for x in range(2):
                for y in range(4):
                    for p in range(2):
                        nearby = stencil(e, fx, fy, fz, x, y, p, None)
                        value = ((1.0 - OMEGA) * e(x, y, p) + bb[x0 + x + 1, y0 + y + 1, p]
                                 + st[x0 + x, y0 + y, p] * nearby) + coarse
                        cc[it, x0 + x - 1, y0 + y - 1, p] = value
                        v_per[x0 + x - 1, y0 + y - 1, p] = v_per[x0 + x - 1, y0 + y - 1, p] + value

        blocks(2, B, 2, B, 2, 4, correct)
        halo(SIDES, h_copy(it), "start")

        if it + 1 == ITERS:
            def unpermute(n, carry):
                for y in range(B):
                    for p in range(2):
                        v_nat[1 + n, 1 + y, pl.ds(p, 8, stride=2), :] = v_per[1 + n, 1 + y, p]
                return carry

            lax.fori_loop(0, B, unpermute, 0)
            out_v = pltpu.make_async_copy(v_nat.at[pl.ds(1, B), pl.ds(1, B)], pot_hbm, loc.at[0])
            out_v.start()

        halo(SIDES, h_copy(it), "here")

        def update(x0, y0):
            e = reader(cc.at[it], x0, y0, 1, 1)
            fx, fy, fz = (reader(k, x0, y0, 2, 2) for k in (kx, ky, kz))
            for x in range(2):
                for y in range(4):
                    for p in range(2):
                        flow = stencil(e, fx, fy, fz, x, y, p, None) - dg[x0 + x + 2, y0 + y + 2, p] * e(x, y, p)
                        value = rr[it, x0 + x + 2, y0 + y + 2, p] + flow
                        if it + 1 < ITERS:
                            rr[it + 1, x0 + x + 2, y0 + y + 2, p] = value
                        else:
                            res_nat[x0 + x, y0 + y, pl.ds(p, 8, stride=2), :] = value

        blocks(0, B, 0, B, 2, 4, update)

    out_r = pltpu.make_async_copy(res_nat, res_hbm, loc.at[1])
    out_r.start()
    out_v.wait()
    out_r.wait()

    halo(AROUND, sig_copy, "sent")
    halo(SIDES, v_copy, "sent")

    def c_sent(k, carry):
        c_copy(k, i).wait_send()
        return carry

    lax.fori_loop(1, NI, c_sent, 0)
    for it in range(ITERS):
        halo(AROUND, r_copy(it), "sent")
        halo(SIDES, h_copy(it), "sent")

        def ag_sent(k, carry):
            ag_copy(it, k, j).wait_send()
            return carry

        lax.fori_loop(1, NJ, ag_sent, 0)

        def rs_sent(k, carry):
            rs_copy(it, k, i).wait_send()
            return carry

        lax.fori_loop(1, NI, rs_sent, 0)


def on_device(start_potentials, conductivity, electrodes, coarse_inverse):
    shape = jax.ShapeDtypeStruct((B, B, B, F), F32)
    tiles = lambda *lead: pltpu.VMEM(tuple(lead) + (2, 8, F), F32)
    dma = pltpu.SemaphoreType.DMA
    anywhere = pl.BlockSpec(memory_space=pl.ANY)
    return pl.pallas_call(
        kernel,
        out_shape=(shape, shape),
        in_specs=[anywhere, anywhere, pl.BlockSpec(memory_space=pltpu.VMEM), anywhere],
        out_specs=(anywhere, anywhere),
        scratch_shapes=[
            pltpu.VMEM((22, 32, 16), F32),
            pltpu.VMEM((16, 32), F32),
            tiles(22, 22),
            pltpu.VMEM((18, 18, 16, F), F32),
            tiles(18, 18),
            tiles(ITERS, 20, 20),
            tiles(22, 22),
            tiles(22, 22),
            tiles(22, 22),
            tiles(ITERS, 18, 18),
            tiles(21, 20),
            tiles(20, 21),
            tiles(20, 20),
            tiles(20, 20),
            tiles(20, 20),
            pltpu.VMEM((16, 16, 16, F), F32),
            pltpu.VMEM((256, 512), F32),
            pltpu.VMEM((ITERS, BLK, F), F32),
            pltpu.VMEM((ITERS, 512, F), F32),
            pltpu.VMEM((ITERS, 256, F), F32),
            pltpu.VMEM((ITERS, NI, BLK, F), F32),
            pltpu.VMEM((128, F), F32),
            pltpu.VMEM((128, F), F32),
            dma((8,)), dma((8,)),
            dma((4,)), dma((4,)),
            dma((NI,)), dma((NI,)),
            dma((ITERS, NJ)), dma((ITERS, NJ)),
            dma((ITERS, NI)), dma((ITERS, NI)),
            dma((ITERS, 8)), dma((ITERS, 8)),
            dma((ITERS, 4)), dma((ITERS, 4)),
            dma((3,)),
        ],
        compiler_params=pltpu.CompilerParams(
            collective_id=0, has_side_effects=True, vmem_limit_bytes=60 * 2**20
        ),
        cost_estimate=pl.CostEstimate(flops=10**8, bytes_accessed=10**7, transcendentals=0),
    )(start_potentials, conductivity, electrodes.T, coarse_inverse)


def solution(mesh):
    in_specs = (P("gx", "gy", None, None), P("gx", "gy", None), P(), P(("gx", "gy"), None))
    out_specs = (P("gx", "gy", None, None), P("gx", "gy", None, None))
    return jax.shard_map(
        on_device, mesh=mesh, in_specs=in_specs, out_specs=out_specs, check_vma=False
    )
```

time: 604 us -> 104 us (0.17)
  waiting for transfers between devices: 340 us -> 0 us
  other arithmetic: 100 us -> 0 us
  Pallas kernels: 0 us -> 98.6 us
  starting transfers between devices: 89.8 us -> 0 us
  local copies, waits for them, and re-layouts: 45.9 us -> 4.57 us
  between operations: 15.4 us -> 0.65 us
  matrix products: 6.06 us -> 0 us
    all_gather x2 -> x0, waiting for transfers between devices: 309 us -> none  [coarse_solve(): lax.all_gather(coarse_res, ('gx', 'gy'), axis=0, tiled=True)]
    pallas_call x0 -> x1, Pallas kernels: none -> 98.6 us  [on_device(): pl.pallas_call(kernel, out_shape=(shape, shape), in_specs=[anywhere, anyw...]
    ppermute x24 -> x0, starting transfers between devices: 89.5 us -> none  [the longest x12 51.9 us: extended(): lax.ppermute(lax.slice_in_dim(block, 0, width, axis=dim), axis, backward)]
    add x11 -> x0, other arithmetic: 64.7 us -> none  [the longest x4 40.1 us: local_solve(): estimate + step_size * (residual_part - apply_op(couplings, widened))]
    ppermute x24 -> x0, waiting for transfers between devices: 31.6 us -> none  [the longest x12 26.7 us: extended(): lax.ppermute(lax.slice_in_dim(block, 0, width, axis=dim), axis, backward)]
    slice x31 -> x0, local copies, waits for them, and re-layouts: 19.1 us -> none  [the longest x9 10.1 us: apply_op(): deeper = jnp.concatenate([values[:, :, 1:], zero_layer], axis=2)]
    sub x3 -> x0, other arithmetic: 16.7 us -> none  [the longest x2 9.54 us: on_device(): residual_own - apply_op(couplings_own, rim_single(correction))]
    mul x5 -> x0, other arithmetic: 11.7 us -> none  [the longest x2 6.41 us: apply_op(): lower_face * deeper]
  transfers between devices with their start and end apart: 26 -> 0, of which waited for: 16 -> 0; matrix products, arithmetic and copies ran while one was open for 18% -> 0% of each run, Pallas kernels for 0% -> 0%
where the time goes in v1:
time: 104 us
  Pallas kernels  98.6 us (95%)
  local copies, waits for them, and re-layouts  4.57 us (4%)
    pallas_call x1, Pallas kernels, on_device(): pl.pallas_call(kernel, out_shape=(shape, shape), in_specs=[anywhere, anyw...  98.6 us
    unnamed x4, local copies, waits for them, and re-layouts  4.57 us

profile of v1, /device:TPU:5, one launch (start us, length us, event | category | flops | bytes accessed | tf_op | source)
XLA Modules:
  0.0 103.8 jit_solution(17021822785184736024)
XLA Ops:
  0.6 98.6 %shard_map.59 = (f32[16,16,16,128]{3,2,1,0:T(8,128)}, f32[16,16,16,128]{3,2,1,0:T(8,128)}) custom-call(f32[16,16,16,128]{3,2,1,0:T(8,128)} %v_hbm.1, f32[16,16,16]{2,1,0:T(8,128)} %cond_ref.1, s32[2,128]{1,0:T(2,128)} %bitcast.1, f32[32,4096]{1,0:T(8,128)} %cinv_hbm.1), custom_call_target="tpu_custom_call" | custom-call | flops 100000000 | bytes 10000000 | tf_op jit(solution)/shard_map/pallas_call | solution.py:514
  99.2 0.0 copy-start
  99.3 3.2 %copy.8 = f32[16,16,16,128]{3,2,1,0:T(8,128)} copy(f32[16,16,16,128]{3,2,1,0:T(8,128)} %get-tuple-element.4) | data formatting | bytes 4194304
  102.5 0.0 copy-done
  102.5 1.3 %copy.9 = f32[16,16,16,128]{3,2,1,0:T(8,128)} copy(f32[16,16,16,128]{3,2,1,0:T(8,128)S(1)} %copy-done) | data formatting | bytes 4194304
Async XLA Ops:
  99.2 3.3 %copy-start = (f32[16,16,16,128]{3,2,1,0:T(8,128)S(1)}, f32[16,16,16,128]{3,2,1,0:T(8,128)}, u32[]{:S(2)}) copy-start(f32[16,16,16,128]{3,2,1,0:T(8,128)} %get-tuple-element.5) | copy-start | bytes 6291460

commit v2 on v1

v2 whole, which is shorter than its diff:
```python
import jax
import jax.numpy as jnp
from jax import lax
from jax.experimental import pallas as pl
from jax.experimental.pallas import tpu as pltpu
from jax.sharding import PartitionSpec as P

OMEGA = 0.7
CURRENT = 8.0
ITERS = 2
NI, NJ = 8, 16
NQ = NJ // 2
B = 16
F = 128
E2 = B + 4
BLK = 32
MESH = pl.DeviceIdType.MESH
F32 = jnp.float32

SIDES = ((-1, 0), (1, 0), (0, -1), (0, 1))
CORNERS = ((-1, -1), (-1, 1), (1, -1), (1, 1))
AROUND = SIDES + CORNERS


def stencil(e, kx, ky, kz, x, y, p):
    total = kx(x, y, p) * e(x - 1, y, p) + kx(x + 1, y, p) * e(x + 1, y, p)
    total = total + (ky(x, y, p) * e(x, y - 1, p) + ky(x, y + 1, p) * e(x, y + 1, p))
    other = e(x, y, 1 - p)
    if p == 0:
        across = pltpu.roll(kz(x, y, 1) * other, 1, 0)
    else:
        across = kz(x, y, 1) * pltpu.roll(other, 7, 0)
    return total + (kz(x, y, 0) * other + across)


def reader(ref, x0, y0, shift):
    held = {}

    def get(x, y, p):
        key = (x, y, p)
        if key not in held:
            held[key] = ref[x0 + (x + shift), y0 + (y + shift), p]
        return held[key]

    return get


def region(body, x_lo, x_n, y_lo, y_n, xb, yb, copies=1, step_x=0, step_y=0):
    nx, ny = x_n // xb, y_n // yb
    assert nx * xb == x_n and ny * yb == y_n
    cells = [(x, y, p) for x in range(xb) for y in range(yb) for p in range(2)]

    def one(n, carry):
        x0, y0 = x_lo, y_lo
        if copies > 1:
            side = n // (nx * ny)
            x0, y0 = x0 + side * step_x, y0 + side * step_y
            n = n % (nx * ny) if nx * ny > 1 else 0
        if nx > 1:
            x0 = x0 + (n // ny) * xb
        if ny > 1:
            y0 = y0 + ((n % ny) if nx > 1 else n) * yb
        body(x0, y0, cells)
        return carry

    lax.fori_loop(0, copies * nx * ny, one, 0)


def kernel(
    v_hbm, cond_ref, elec_ref, cinv_hbm,
    pot_hbm, res_hbm,
    sig, sig_t, v_nat, uu, rr, bb, e_a, e_b, kx, ky, kz, st, dg, res_nat,
    cblk, crow, gath, part, recv, pro, acc,
    sig_s, sig_r, u_s, u_r, c_s, c_r, ag_s, ag_r, tw_s, tw_r, rs_s, rs_r, loc,
):
    i = lax.axis_index("gx")
    j = lax.axis_index("gy")
    core = lax.rem(j, 2)
    pair = j // 2
    sig_b = uu.at[ITERS]

    def there(dx, dy):
        ok = None
        for d, pos, n in ((dx, i, NI), (dy, j, NJ)):
            if d:
                term = (pos > 0) if d < 0 else (pos < n - 1)
                ok = term if ok is None else ok & term
        return ok

    bar = pltpu.get_barrier_semaphore()

    def greet(to_i, to_j):
        pl.semaphore_signal(bar, inc=1, device_id=(to_i, to_j), device_id_type=MESH)

    count = jnp.int32(NI - 1 + NQ - 1)
    for dx, dy in ((0, -1), (0, 1)) + CORNERS:
        ok = there(dx, dy)

        @pl.when(ok)
        def _():
            greet(i + dx, j + dy)

        count = count + jnp.where(ok, 1, 0)

    def greet_j(k, carry):
        greet(i, lax.rem(j + 2 * k, NJ))
        return carry

    def greet_i(k, carry):
        greet(lax.rem(i + k, NI), j)
        return carry

    lax.fori_loop(1, NQ, greet_j, 0)
    lax.fori_loop(1, NI, greet_i, 0)

    own_s = pltpu.make_async_copy(cond_ref, sig.at[pl.ds(3, B), pl.ds(8, B)], loc.at[2])
    own_s.start()
    own_v = pltpu.make_async_copy(v_hbm, v_nat, loc.at[0])
    own_v.start()
    own_c = pltpu.make_async_copy(
        cinv_hbm.at[:, pl.ds(i * 512, 512)], cblk.at[pl.ds(i * BLK, BLK)], loc.at[1]
    )
    own_c.start()

    def halo(dirs, make, what):
        for n, (dx, dy) in enumerate(dirs):
            if what in ("start", "sent"):

                @pl.when(there(dx, dy))
                def _():
                    copy = make(n, dx, dy)
                    copy.start() if what == "start" else copy.wait_send()

            else:

                @pl.when(there(-dx, -dy))
                def _():
                    make(n, dx, dy).wait_recv()

    def sig_copy(n, dx, dy):
        xs = {-1: (3, 3, 19), 0: (3, 16, 3), 1: (16, 3, 0)}[dx]
        ys = {-1: (8, 8, 24), 0: (8, 16, 8), 1: (16, 8, 0)}[dy]
        src = cond_ref.at[pl.ds(xs[0] - 3, xs[1]), pl.ds(ys[0] - 8, ys[1])]
        dst = sig.at[pl.ds(xs[2], xs[1]), pl.ds(ys[2], ys[1])]
        return pltpu.make_async_remote_copy(
            src_ref=src, dst_ref=dst, send_sem=sig_s.at[n], recv_sem=sig_r.at[n],
            device_id=(i + dx, j + dy), device_id_type=MESH)

    def u_copy(level, base, x_layers, y_layers):
        def span(d, layers):
            if d == 0:
                return 3, B, 3
            first, number = layers
            start = 3 + first if d < 0 else 3 + B - first - number
            return start, number, start - d * B

        def make(n, dx, dy):
            xs, ys = span(dx, x_layers), span(dy, y_layers)
            return pltpu.make_async_remote_copy(
                src_ref=uu.at[level, pl.ds(xs[0], xs[1]), pl.ds(ys[0], ys[1])],
                dst_ref=uu.at[level, pl.ds(xs[2], xs[1]), pl.ds(ys[2], ys[1])],
                send_sem=u_s.at[level, base + n], recv_sem=u_r.at[level, base + n],
                device_id=(i + dx, j + dy), device_id_type=MESH)

        return make

    def near(level, what):
        halo(SIDES, u_copy(level, 0, (0, 1), (0, 1)), what)

    def far(level, what):
        halo(SIDES, u_copy(level, 4, (1, 2), (1, 2)), what)
        halo(CORNERS, u_copy(level, 8, (0, 2), (0, 3)), what)
        halo(CORNERS, u_copy(level, 12, (2, 1), (0, 1)), what)

    def c_copy(k, source):
        to = lax.rem(i + k, NI)
        return pltpu.make_async_remote_copy(
            src_ref=cinv_hbm.at[:, pl.ds(to * 512, 512)],
            dst_ref=cblk.at[pl.ds(source * BLK, BLK)],
            send_sem=c_s.at[k], recv_sem=c_r.at[k],
            device_id=(to, j), device_id_type=MESH)

    def ag_copy(it, k, source):
        return pltpu.make_async_remote_copy(
            src_ref=crow.at[it],
            dst_ref=gath.at[it, source, core],
            send_sem=ag_s.at[it, k], recv_sem=ag_r.at[it, k],
            device_id=(i, lax.rem(j + 2 * k, NJ)), device_id_type=MESH)

    def twin_copy(it, which):
        return pltpu.make_async_remote_copy(
            src_ref=gath.at[it, :, which], dst_ref=gath.at[it, :, which],
            send_sem=tw_s.at[it], recv_sem=tw_r.at[it],
            device_id=(i, j + 1 - 2 * core), device_id_type=MESH)

    def rs_copy(it, k, source):
        to = lax.rem(i + k, NI)
        return pltpu.make_async_remote_copy(
            src_ref=part.at[it, pl.ds(to * BLK, BLK)],
            dst_ref=recv.at[it, source],
            send_sem=rs_s.at[it, k], recv_sem=rs_r.at[it, k],
            device_id=(to, j), device_id_type=MESH)

    for dx, dy in AROUND:

        @pl.when(~there(dx, dy))
        def _():
            xs = {-1: (0, 3), 0: (3, 16), 1: (19, 3)}[dx]
            ys = {-1: (0, 8), 0: (8, 16), 1: (24, 8)}[dy]
            sig[pl.ds(*xs), pl.ds(*ys)] = jnp.zeros((xs[1], ys[1], 16), F32)

    def spread(columns, copies, inner):
        def one(n, carry):
            x = copies[0] + n + (n // copies[1]) * copies[2]
            if inner:
                sig_t[:, 8 : 8 + B] = jnp.transpose(sig[x, 8 : 8 + B])
            else:
                sig_t[...] = jnp.transpose(sig[x])
            for p in range(2):
                rows = sig_t[pl.ds(p, 8, stride=2), :]
                for y in columns:
                    sig_b[x, y, p] = jnp.broadcast_to(rows[:, y + 5 : y + 6], (8, F))
            return carry

        return one

    own_s.wait()
    lax.fori_loop(0, B, spread(range(3, 3 + B), (3, B, 0), True), 0)

    level = lax.broadcasted_iota(jnp.int32, (8, F), 0)

    def faces(x0, y0, cells):
        s = reader(sig_b, x0, y0, 1)
        done = {}
        for x, y, p in cells:
            if p:
                continue
            even, odd = s(x, y, 0), s(x, y, 1)
            kz_in = 0.5 * (even + odd)
            next_even = jnp.where(level < 7, pltpu.roll(even, 7, 0), 0.0)
            bottom = 0.5 * (odd + next_even)
            kz_out = jnp.where(level < 7, bottom, 0.0)
            above = pltpu.roll(kz_out, 1, 0)
            for q in range(2):
                west = 0.5 * (s(x, y, q) + s(x - 1, y, q))
                east = 0.5 * (s(x, y, q) + s(x + 1, y, q))
                south = 0.5 * (s(x, y, q) + s(x, y - 1, q))
                north = 0.5 * (s(x, y, q) + s(x, y + 1, q))
                depth = (kz_in + above) if q == 0 else (kz_in + bottom)
                d = west + east + south + north + depth
                step = jnp.where(s(x, y, q) > 0.0, OMEGA / jnp.maximum(d, 1e-30), 0.0)
                done[x, y, q] = west, south, (kz_in, kz_out)[q], d, step
        for (x, y, p), values in done.items():
            for ref, value in zip((kx, ky, kz, dg, st), values):
                ref[x0 + x, y0 + y, p] = value

    region(faces, 3, 14, 3, 14, 7, 2)

    own_v.wait()

    def permute(n, carry):
        for y in range(B):
            for p in range(2):
                uu[0, 3 + n, 3 + y, p] = v_nat[n, y, pl.ds(p, 8, stride=2), :]
        return carry

    lax.fori_loop(0, B, permute, 0)

    pl.semaphore_wait(bar, count)
    halo(AROUND, sig_copy, "start")
    near(0, "start")
    far(0, "start")

    def c_start(k, carry):
        c_copy(k, i).start()
        return carry

    lax.fori_loop(1, NI, c_start, 0)

    for dx, dy in AROUND:

        @pl.when(~there(dx, dy))
        def _():
            xr = {-1: (0, 3), 0: (3, B), 1: (B + 3, 3)}[dx]
            yr = {-1: (0, 3), 0: (3, B), 1: (B + 3, 3)}[dy]

            def zero_u(n, carry):
                for w in range(ITERS):
                    uu[w, xr[0] + n // yr[1], yr[0] + n % yr[1]] = jnp.zeros((2, 8, F), F32)
                return carry

            lax.fori_loop(0, xr[1] * yr[1], zero_u, 0)

    def zero_ring(n, carry):
        zero = jnp.zeros((2, 8, F), F32)
        bb[0, n] = zero
        bb[E2 + 1, n] = zero
        bb[n, 0] = zero
        bb[n, E2 + 1] = zero
        return carry

    lax.fori_loop(0, E2 + 2, zero_ring, 0)

    corner = (i * B - 2) * (NJ * B) + (j * B - 2)
    source = elec_ref[0:1, :]
    sink = elec_ref[1:2, :]

    def residual(n):
        def body(x0, y0, cells):
            e = reader(uu.at[n], x0, y0, 1)
            fx, fy, fz = (reader(k, x0, y0, 0) for k in (kx, ky, kz))
            done = {}
            for x, y, p in cells:
                value = stencil(e, fx, fy, fz, x, y, p) - dg[x0 + x, y0 + y, p] * e(x, y, p)
                if n > 0:
                    value = rr[x0 + x, y0 + y, p] + value
                elif p == 0:
                    here = corner + (x0 + x) * (NJ * B) + (y0 + y)
                    force = jnp.where(source == here, CURRENT, 0.0) - jnp.where(sink == here, CURRENT, 0.0)
                    value = value + jnp.where(level == 0, jnp.broadcast_to(force, (8, F)), 0.0)
                done[x, y, p] = value, (st[x0 + x, y0 + y, p] * value if n < ITERS else None)
            for (x, y, p), (value, first) in done.items():
                if n < ITERS:
                    rr[x0 + x, y0 + y, p] = value
                    bb[x0 + x + 1, y0 + y + 1, p] = first
                else:
                    res_nat[x0 + x - 2, y0 + y - 2, pl.ds(p, 8, stride=2), :] = value

        return body

    def residual_own_rim(n):
        region(residual(n), 2, 1, 2, 16, 1, 16, 2, 15, 0)
        region(residual(n), 3, 14, 2, 1, 14, 1, 2, 0, 15)

    halo(AROUND, sig_copy, "here")
    lax.fori_loop(0, 6, spread(range(E2 + 2), (0, 3, 16), False), 0)
    lax.fori_loop(0, B, spread((0, 1, 2, 19, 20, 21), (3, B, 0), False), 0)
    region(faces, 0, 3, 0, 20, 3, 10, 2, 17, 0)
    region(faces, 3, 14, 0, 3, 7, 3, 2, 0, 17)

    def last_faces(n, carry):
        for p in range(2):
            kx[E2, n, p] = 0.5 * (sig_b[E2 + 1, n + 1, p] + sig_b[E2, n + 1, p])
            ky[n, E2, p] = 0.5 * (sig_b[n + 1, E2 + 1, p] + sig_b[n + 1, E2, p])
        return carry

    lax.fori_loop(0, E2, last_faces, 0)

    for dx, dy in SIDES:

        @pl.when(~there(dx, dy))
        def _():
            def zero_last(n, carry):
                x = {-1: 2, 0: 3 + n, 1: B + 3}[dx]
                y = {-1: 2, 0: 3 + n, 1: B + 3}[dy]
                uu[ITERS, x, y] = jnp.zeros((2, 8, F), F32)
                return carry

            lax.fori_loop(0, B, zero_last, 0)

    def sweep(src, shift, store):
        def body(x0, y0, cells):
            e = reader(src, x0, y0, shift)
            fx, fy, fz = (reader(k, x0, y0, 0) for k in (kx, ky, kz))
            done = {}
            for x, y, p in cells:
                nearby = stencil(e, fx, fy, fz, x, y, p)
                done[x, y, p] = ((1.0 - OMEGA) * e(x, y, p) + bb[x0 + x + 1, y0 + y + 1, p]
                                 + st[x0 + x, y0 + y, p] * nearby)
            for (x, y, p), value in done.items():
                store(x0 + x, y0 + y, p, value)

        return body

    def into_a(x, y, p, value):
        e_a[x, y, p] = value

    def into_b(x, y, p, value):
        e_b[x, y, p] = value

    def coarse_at(x, y):
        block = ((x - 2) // 4) * 4 + (y - 2) // 4
        return pro[pl.ds(pl.multiple_of(block * 8, 8), 8), :]

    for it in range(ITERS):
        region(residual(it), 3, 14, 3, 14, 7, 2)
        near(it, "here")
        residual_own_rim(it)

        def restrict(n, carry):
            a, b = n // 4, n % 4
            tiles = [rr[2 + 4 * a + x, 2 + 4 * b + y, p] for x in range(4) for y in range(4) for p in range(2)]
            while len(tiles) > 1:
                tiles = [one + two for one, two in zip(tiles[::2], tiles[1::2])]
            acc[pl.ds(pl.multiple_of(n * 8, 8), 8), :] = tiles[0]
            return carry

        lax.fori_loop(0, 16, restrict, 0)
        rows = acc[pl.ds(0, BLK, stride=4), :]
        for q in range(1, 4):
            rows = rows + acc[pl.ds(q, BLK, stride=4), :]
        crow[it] = rows
        gath[it, pair, core] = rows

        def ag_start(k, carry):
            ag_copy(it, k, pair).start()
            return carry

        lax.fori_loop(1, NQ, ag_start, 0)

        region(sweep(bb, 1, into_a), 3, 14, 3, 14, 7, 2)
        region(sweep(e_a, 0, into_b), 4, 12, 4, 12, 6, 3)

        def ag_wait(k, carry):
            ag_copy(it, k, lax.rem(pair - k + NQ, NQ)).wait_recv()
            return carry

        lax.fori_loop(1, NQ, ag_wait, 0)
        twin_copy(it, core).start()

        def into_u(x, y, p, value):
            uu[it + 1, x + 1, y + 1, p] = value

        region(sweep(e_b, 0, into_u), 5, 10, 5, 10, 5, 5)

        if it == 0:
            own_c.wait()

            def c_wait(k, carry):
                c_copy(k, lax.rem(i - k + NI, NI)).wait_recv()
                return carry

            lax.fori_loop(1, NI, c_wait, 0)

        twin_copy(it, 1 - core).wait_recv()
        part[it] = jnp.dot(
            cblk[...], gath[it].reshape(512, F), precision=lax.Precision.HIGHEST, preferred_element_type=F32
        )

        def rs_start(k, carry):
            rs_copy(it, k, i).start()
            return carry

        lax.fori_loop(1, NI, rs_start, 0)

        far(it, "here")
        region(residual(it), 0, 2, 0, 20, 2, 10, 2, 18, 0)
        region(residual(it), 2, 16, 0, 2, 8, 2, 2, 0, 18)
        region(sweep(bb, 1, into_a), 0, 3, 0, 20, 3, 10, 2, 17, 0)
        region(sweep(bb, 1, into_a), 3, 14, 0, 3, 7, 3, 2, 0, 17)
        region(sweep(e_a, 0, into_b), 1, 3, 1, 18, 3, 9, 2, 15, 0)
        region(sweep(e_a, 0, into_b), 4, 12, 1, 3, 6, 3, 2, 0, 15)

        def rs_wait(k, carry):
            rs_copy(it, k, lax.rem(i - k + NI, NI)).wait_recv()
            return carry

        lax.fori_loop(1, NI, rs_wait, 0)
        recv[it, i] = part[it, pl.ds(pl.multiple_of(i * BLK, BLK), BLK)]
        total = recv[it, 0]
        for q in range(1, NI):
            total = total + recv[it, q]
        for q in range(4):
            pro[pl.ds(q, BLK, stride=4), :] = total

        def into_u_coarse(x, y, p, value):
            uu[it + 1, x + 1, y + 1, p] = value + coarse_at(x, y)

        region(sweep(e_b, 0, into_u_coarse), 2, 3, 2, 16, 3, 8, 2, 13, 0)
        region(sweep(e_b, 0, into_u_coarse), 5, 10, 2, 3, 10, 3, 2, 0, 13)
        near(it + 1, "start")
        if it + 1 < ITERS:
            far(it + 1, "start")

        def add_coarse(x0, y0, cells):
            done = {}
            for x, y, p in cells:
                done[x, y, p] = uu[it + 1, x0 + x + 1, y0 + y + 1, p] + coarse_at(x0 + x, y0 + y)
            for (x, y, p), value in done.items():
                uu[it + 1, x0 + x + 1, y0 + y + 1, p] = value

        region(add_coarse, 5, 10, 5, 10, 5, 2)

    def potentials(x0, y0, cells):
        done = {}
        for x, y, p in cells:
            total = uu[0, x0 + x + 1, y0 + y + 1, p]
            for n in range(ITERS):
                total = total + uu[n + 1, x0 + x + 1, y0 + y + 1, p]
            done[x, y, p] = total
        for (x, y, p), value in done.items():
            v_nat[x0 + x - 2, y0 + y - 2, pl.ds(p, 8, stride=2), :] = value

    region(potentials, 2, B, 2, B, 4, 4)
    out_v = pltpu.make_async_copy(v_nat, pot_hbm, loc.at[0])
    out_v.start()
    region(residual(ITERS), 3, 14, 3, 14, 7, 2)
    near(ITERS, "here")
    residual_own_rim(ITERS)
    out_r = pltpu.make_async_copy(res_nat, res_hbm, loc.at[1])
    out_r.start()
    out_v.wait()

    halo(AROUND, sig_copy, "sent")

    def c_sent(k, carry):
        c_copy(k, i).wait_send()
        return carry

    lax.fori_loop(1, NI, c_sent, 0)
    near(ITERS, "sent")
    for it in range(ITERS):
        near(it, "sent")
        far(it, "sent")
        twin_copy(it, core).wait_send()

        def ag_sent(k, carry):
            ag_copy(it, k, pair).wait_send()
            return carry

        lax.fori_loop(1, NQ, ag_sent, 0)

        def rs_sent(k, carry):
            rs_copy(it, k, i).wait_send()
            return carry

        lax.fori_loop(1, NI, rs_sent, 0)
    out_r.wait()


def on_device(start_potentials, conductivity, electrodes, coarse_inverse):
    shape = jax.ShapeDtypeStruct((B, B, B, F), F32)
    tiles = lambda *lead: pltpu.VMEM(tuple(lead) + (2, 8, F), F32)
    dma = pltpu.SemaphoreType.DMA
    anywhere = pl.BlockSpec(memory_space=pl.ANY)
    return pl.pallas_call(
        kernel,
        out_shape=(shape, shape),
        in_specs=[anywhere, anywhere, pl.BlockSpec(memory_space=pltpu.VMEM), anywhere],
        out_specs=(anywhere, anywhere),
        scratch_shapes=[
            pltpu.VMEM((22, 32, 16), F32),
            pltpu.VMEM((16, 32), F32),
            pltpu.VMEM((B, B, 16, F), F32),
            tiles(ITERS + 1, 22, 22),
            tiles(20, 20),
            tiles(22, 22),
            tiles(20, 20),
            tiles(20, 20),
            tiles(21, 20),
            tiles(20, 21),
            tiles(20, 20),
            tiles(20, 20),
            tiles(20, 20),
            pltpu.VMEM((B, B, 16, F), F32),
            pltpu.VMEM((256, 512), F32),
            pltpu.VMEM((ITERS, BLK, F), F32),
            pltpu.VMEM((ITERS, NQ, 2, BLK, F), F32),
            pltpu.VMEM((ITERS, 256, F), F32),
            pltpu.VMEM((ITERS, NI, BLK, F), F32),
            pltpu.VMEM((128, F), F32),
            pltpu.VMEM((128, F), F32),
            dma((8,)), dma((8,)),
            dma((ITERS + 1, 16)), dma((ITERS + 1, 16)),
            dma((NI,)), dma((NI,)),
            dma((ITERS, NQ)), dma((ITERS, NQ)),
            dma((ITERS,)), dma((ITERS,)),
            dma((ITERS, NI)), dma((ITERS, NI)),
            dma((3,)),
        ],
        compiler_params=pltpu.CompilerParams(
            collective_id=0, has_side_effects=True, vmem_limit_bytes=56 * 2**20
        ),
        cost_estimate=pl.CostEstimate(flops=10**8, bytes_accessed=10**7, transcendentals=0),
    )(start_potentials, conductivity, electrodes.T, coarse_inverse)


def solution(mesh):
    in_specs = (P("gx", "gy", None, None), P("gx", "gy", None), P(), P(("gx", "gy"), None))
    out_specs = (P("gx", "gy", None, None), P("gx", "gy", None, None))
    return jax.shard_map(
        on_device, mesh=mesh, in_specs=in_specs, out_specs=out_specs, check_vma=False
    )
```

time: 104 us -> 96.6 us (0.929)
  Pallas kernels: 98.6 us -> 91.3 us
    pallas_call x1, Pallas kernels: 98.6 us -> 91.3 us  [on_device(): pl.pallas_call(kernel, out_shape=(shape, shape), in_specs=[anywhere, anyw...]
where the time goes in v2:
time: 96.6 us; the launch traced here: 96.5 us
  Pallas kernels  91.3 us (95%)
  local copies, waits for them, and re-layouts  4.57 us (5%)
    pallas_call x1, Pallas kernels, on_device(): pl.pallas_call(kernel, out_shape=(shape, shape), in_specs=[anywhere, anyw...  91.3 us
    unnamed x4, local copies, waits for them, and re-layouts  4.57 us

profile of v2, /device:TPU:5, one launch (start us, length us, event | category | flops | bytes accessed | tf_op | source)
XLA Modules:
  0.0 96.5 jit_solution(7863940100755666722)
XLA Ops:
  0.6 91.3 %shard_map.59 = (f32[16,16,16,128]{3,2,1,0:T(8,128)}, f32[16,16,16,128]{3,2,1,0:T(8,128)}) custom-call(f32[16,16,16,128]{3,2,1,0:T(8,128)} %v_hbm.1, f32[16,16,16]{2,1,0:T(8,128)} %cond_ref.1, s32[2,128]{1,0:T(2,128)} %bitcast.1, f32[32,4096]{1,0:T(8,128)} %cinv_hbm.1), custom_call_target="tpu_custom_call" | custom-call | flops 100000000 | bytes 10000000 | tf_op jit(solution)/shard_map/pallas_call | solution.py:536
  91.9 0.0 copy-start
  91.9 3.2 %copy.8 = f32[16,16,16,128]{3,2,1,0:T(8,128)} copy(f32[16,16,16,128]{3,2,1,0:T(8,128)} %get-tuple-element.4) | data formatting | bytes 4194304
  95.1 0.0 copy-done
  95.1 1.3 %copy.9 = f32[16,16,16,128]{3,2,1,0:T(8,128)} copy(f32[16,16,16,128]{3,2,1,0:T(8,128)S(1)} %copy-done) | data formatting | bytes 4194304
Async XLA Ops:
  91.9 3.3 %copy-start = (f32[16,16,16,128]{3,2,1,0:T(8,128)S(1)}, f32[16,16,16,128]{3,2,1,0:T(8,128)}, u32[]{:S(2)}) copy-start(f32[16,16,16,128]{3,2,1,0:T(8,128)} %get-tuple-element.5) | copy-start | bytes 6291460

commit v3 on v2

--- a/solution.py
+++ b/solution.py
@@ -9,7 +9,7 @@
 CURRENT = 8.0
 ITERS = 2
 NI, NJ = 8, 16
-NQ = NJ // 2
+NK, NR = 8, 16
 B = 16
 F = 128
 E2 = B + 4
@@ -68,15 +68,17 @@
 
 def kernel(
     v_hbm, cond_ref, elec_ref, cinv_hbm,
-    pot_hbm, res_hbm,
-    sig, sig_t, v_nat, uu, rr, bb, e_a, e_b, kx, ky, kz, st, dg, res_nat,
+    v_nat, res_nat,
+    sig, sig_t, uu, rr, bb, e_a, e_b, kx, ky, kz, st, dg,
     cblk, crow, gath, part, recv, pro, acc,
-    sig_s, sig_r, u_s, u_r, c_s, c_r, ag_s, ag_r, tw_s, tw_r, rs_s, rs_r, loc,
+    sig_s, sig_r, u_s, u_r, c_s, c_r, ag_s, ag_r, rs_s, rs_r, loc,
 ):
     i = lax.axis_index("gx")
     j = lax.axis_index("gy")
-    core = lax.rem(j, 2)
-    pair = j // 2
+    high, y_at = i // 4, lax.rem(i, 4)
+    z_at, low = j // 4, lax.rem(j, 4)
+    k_at = high * 4 + low
+    r_at = y_at * 4 + z_at
     sig_b = uu.at[ITERS]
 
     def there(dx, dy):
@@ -92,9 +94,21 @@
     def greet(to_i, to_j):
         pl.semaphore_signal(bar, inc=1, device_id=(to_i, to_j), device_id_type=MESH)
 
-    count = jnp.int32(NI - 1 + NQ - 1)
-    for dx, dy in ((0, -1), (0, 1)) + CORNERS:
+    def k_peer(k):
+        to = lax.rem(k_at + k, NK)
+        return to, ((to // 4) * 4 + y_at, z_at * 4 + lax.rem(to, 4))
+
+    def r_peer(k):
+        to = lax.rem(r_at + k, NR)
+        return to, (high * 4 + to // 4, lax.rem(to, 4) * 4 + low)
+
+    count = jnp.int32(NK - 1 + NR - 1)
+    for dx, dy in AROUND:
         ok = there(dx, dy)
+        if dy == 0:
+            ok = ok & ((i + dx) // 4 != high)
+        if dx == 0:
+            ok = ok & ((j + dy) // 4 != z_at)
 
         @pl.when(ok)
         def _():
@@ -102,25 +116,31 @@
 
         count = count + jnp.where(ok, 1, 0)
 
-    def greet_j(k, carry):
-        greet(i, lax.rem(j + 2 * k, NJ))
-        return carry
-
-    def greet_i(k, carry):
-        greet(lax.rem(i + k, NI), j)
-        return carry
-
-    lax.fori_loop(1, NQ, greet_j, 0)
-    lax.fori_loop(1, NI, greet_i, 0)
+    def greet_k(k, carry):
+        greet(*k_peer(k)[1])
+        return carry
+
+    def greet_r(k, carry):
+        greet(*r_peer(k)[1])
+        return carry
+
+    lax.fori_loop(1, NK, greet_k, 0)
+    lax.fori_loop(1, NR, greet_r, 0)
 
     own_s = pltpu.make_async_copy(cond_ref, sig.at[pl.ds(3, B), pl.ds(8, B)], loc.at[2])
     own_s.start()
-    own_v = pltpu.make_async_copy(v_hbm, v_nat, loc.at[0])
+    own_v = pltpu.make_async_copy(v_hbm, v_nat, loc.at[3])
     own_v.start()
-    own_c = pltpu.make_async_copy(
-        cinv_hbm.at[:, pl.ds(i * 512, 512)], cblk.at[pl.ds(i * BLK, BLK)], loc.at[1]
-    )
-    own_c.start()
+    own_c = [
+        pltpu.make_async_copy(
+            cinv_hbm.at[:, pl.ds(pl.multiple_of(h * 2048 + r_at * 128, 128), 128)],
+            cblk.at[pl.ds(r_at * BLK, BLK), pl.ds(h * 128, 128)],
+            loc.at[h],
+        )
+        for h in range(2)
+    ]
+    for copy in own_c:
+        copy.start()
 
     def halo(dirs, make, what):
         for n, (dx, dy) in enumerate(dirs):
@@ -167,39 +187,44 @@
     def near(level, what):
         halo(SIDES, u_copy(level, 0, (0, 1), (0, 1)), what)
 
+    def far_x(level, what):
+        halo(SIDES[:2], u_copy(level, 4, (1, 2), (1, 2)), what)
+
+    def far_y(level, what):
+        halo(SIDES[2:], u_copy(level, 6, (1, 2), (1, 2)), what)
+
     def far(level, what):
-        halo(SIDES, u_copy(level, 4, (1, 2), (1, 2)), what)
+        if what != "start":
+            far_x(level, what)
+            far_y(level, what)
+            far_c(level, what)
+
+    def far_c(level, what):
         halo(CORNERS, u_copy(level, 8, (0, 2), (0, 3)), what)
         halo(CORNERS, u_copy(level, 12, (2, 1), (0, 1)), what)
 
-    def c_copy(k, source):
-        to = lax.rem(i + k, NI)
+    def c_copy(k, h, source):
+        to, device = r_peer(k)
         return pltpu.make_async_remote_copy(
-            src_ref=cinv_hbm.at[:, pl.ds(to * 512, 512)],
-            dst_ref=cblk.at[pl.ds(source * BLK, BLK)],
-            send_sem=c_s.at[k], recv_sem=c_r.at[k],
-            device_id=(to, j), device_id_type=MESH)
+            src_ref=cinv_hbm.at[:, pl.ds(pl.multiple_of(h * 2048 + to * 128, 128), 128)],
+            dst_ref=cblk.at[pl.ds(source * BLK, BLK), pl.ds(h * 128, 128)],
+            send_sem=c_s.at[h, k], recv_sem=c_r.at[h, k],
+            device_id=device, device_id_type=MESH)
 
     def ag_copy(it, k, source):
         return pltpu.make_async_remote_copy(
             src_ref=crow.at[it],
-            dst_ref=gath.at[it, source, core],
+            dst_ref=gath.at[it, pl.ds(source * BLK, BLK)],
             send_sem=ag_s.at[it, k], recv_sem=ag_r.at[it, k],
-            device_id=(i, lax.rem(j + 2 * k, NJ)), device_id_type=MESH)
-
-    def twin_copy(it, which):
-        return pltpu.make_async_remote_copy(
-            src_ref=gath.at[it, :, which], dst_ref=gath.at[it, :, which],
-            send_sem=tw_s.at[it], recv_sem=tw_r.at[it],
-            device_id=(i, j + 1 - 2 * core), device_id_type=MESH)
+            device_id=k_peer(k)[1], device_id_type=MESH)
 
     def rs_copy(it, k, source):
-        to = lax.rem(i + k, NI)
+        to, device = r_peer(k)
         return pltpu.make_async_remote_copy(
             src_ref=part.at[it, pl.ds(to * BLK, BLK)],
             dst_ref=recv.at[it, source],
             send_sem=rs_s.at[it, k], recv_sem=rs_r.at[it, k],
-            device_id=(to, j), device_id_type=MESH)
+            device_id=device, device_id_type=MESH)
 
     for dx, dy in AROUND:
 
@@ -269,13 +294,15 @@
     pl.semaphore_wait(bar, count)
     halo(AROUND, sig_copy, "start")
     near(0, "start")
-    far(0, "start")
+    far_x(0, "start")
+    far_c(0, "start")
 
     def c_start(k, carry):
-        c_copy(k, i).start()
-        return carry
-
-    lax.fori_loop(1, NI, c_start, 0)
+        for h in range(2):
+            c_copy(k, h, r_at).start()
+        return carry
+
+    lax.fori_loop(1, NR, c_start, 0)
 
     for dx, dy in AROUND:
 
@@ -400,23 +427,21 @@
         for q in range(1, 4):
             rows = rows + acc[pl.ds(q, BLK, stride=4), :]
         crow[it] = rows
-        gath[it, pair, core] = rows
+        gath[it, pl.ds(pl.multiple_of(k_at * BLK, BLK), BLK)] = rows
 
         def ag_start(k, carry):
-            ag_copy(it, k, pair).start()
-            return carry
-
-        lax.fori_loop(1, NQ, ag_start, 0)
+            ag_copy(it, k, k_at).start()
+            return carry
+
+        lax.fori_loop(1, NK, ag_start, 0)
+        far_y(it, "start")
 
         region(sweep(bb, 1, into_a), 3, 14, 3, 14, 7, 2)
         region(sweep(e_a, 0, into_b), 4, 12, 4, 12, 6, 3)
 
         def ag_wait(k, carry):
-            ag_copy(it, k, lax.rem(pair - k + NQ, NQ)).wait_recv()
-            return carry
-
-        lax.fori_loop(1, NQ, ag_wait, 0)
-        twin_copy(it, core).start()
+            ag_copy(it, k, lax.rem(k_at - k + NK, NK)).wait_recv()
+            return carry
 
         def into_u(x, y, p, value):
             uu[it + 1, x + 1, y + 1, p] = value
@@ -424,24 +449,26 @@
         region(sweep(e_b, 0, into_u), 5, 10, 5, 10, 5, 5)
 
         if it == 0:
-            own_c.wait()
+            for copy in own_c:
+                copy.wait()
 
             def c_wait(k, carry):
-                c_copy(k, lax.rem(i - k + NI, NI)).wait_recv()
+                for h in range(2):
+                    c_copy(k, h, lax.rem(r_at - k + NR, NR)).wait_recv()
                 return carry
 
-            lax.fori_loop(1, NI, c_wait, 0)
-
-        twin_copy(it, 1 - core).wait_recv()
+            lax.fori_loop(1, NR, c_wait, 0)
+
+        lax.fori_loop(1, NK, ag_wait, 0)
         part[it] = jnp.dot(
-            cblk[...], gath[it].reshape(512, F), precision=lax.Precision.HIGHEST, preferred_element_type=F32
+            cblk[...], gath[it], precision=lax.Precision.HIGHEST, preferred_element_type=F32
         )
 
         def rs_start(k, carry):
-            rs_copy(it, k, i).start()
-            return carry
-
-        lax.fori_loop(1, NI, rs_start, 0)
+            rs_copy(it, k, r_at).start()
+            return carry
+
+        lax.fori_loop(1, NR, rs_start, 0)
 
         far(it, "here")
         region(residual(it), 0, 2, 0, 20, 2, 10, 2, 18, 0)
@@ -452,13 +479,13 @@
         region(sweep(e_a, 0, into_b), 4, 12, 1, 3, 6, 3, 2, 0, 15)
 
         def rs_wait(k, carry):
-            rs_copy(it, k, lax.rem(i - k + NI, NI)).wait_recv()
-            return carry
-
-        lax.fori_loop(1, NI, rs_wait, 0)
-        recv[it, i] = part[it, pl.ds(pl.multiple_of(i * BLK, BLK), BLK)]
+            rs_copy(it, k, lax.rem(r_at - k + NR, NR)).wait_recv()
+            return carry
+
+        lax.fori_loop(1, NR, rs_wait, 0)
+        recv[it, r_at] = part[it, pl.ds(pl.multiple_of(r_at * BLK, BLK), BLK)]
         total = recv[it, 0]
-        for q in range(1, NI):
+        for q in range(1, NR):
             total = total + recv[it, q]
         for q in range(4):
             pro[pl.ds(q, BLK, stride=4), :] = total
@@ -470,7 +497,8 @@
         region(sweep(e_b, 0, into_u_coarse), 5, 10, 2, 3, 10, 3, 2, 0, 13)
         near(it + 1, "start")
         if it + 1 < ITERS:
-            far(it + 1, "start")
+            far_x(it + 1, "start")
+            far_c(it + 1, "start")
 
         def add_coarse(x0, y0, cells):
             done = {}
@@ -492,44 +520,38 @@
             v_nat[x0 + x - 2, y0 + y - 2, pl.ds(p, 8, stride=2), :] = value
 
     region(potentials, 2, B, 2, B, 4, 4)
-    out_v = pltpu.make_async_copy(v_nat, pot_hbm, loc.at[0])
-    out_v.start()
     region(residual(ITERS), 3, 14, 3, 14, 7, 2)
     near(ITERS, "here")
     residual_own_rim(ITERS)
-    out_r = pltpu.make_async_copy(res_nat, res_hbm, loc.at[1])
-    out_r.start()
-    out_v.wait()
 
     halo(AROUND, sig_copy, "sent")
 
     def c_sent(k, carry):
-        c_copy(k, i).wait_send()
-        return carry
-
-    lax.fori_loop(1, NI, c_sent, 0)
+        for h in range(2):
+            c_copy(k, h, r_at).wait_send()
+        return carry
+
+    lax.fori_loop(1, NR, c_sent, 0)
     near(ITERS, "sent")
     for it in range(ITERS):
         near(it, "sent")
         far(it, "sent")
-        twin_copy(it, core).wait_send()
 
         def ag_sent(k, carry):
-            ag_copy(it, k, pair).wait_send()
-            return carry
-
-        lax.fori_loop(1, NQ, ag_sent, 0)
+            ag_copy(it, k, k_at).wait_send()
+            return carry
+
+        lax.fori_loop(1, NK, ag_sent, 0)
 
         def rs_sent(k, carry):
-            rs_copy(it, k, i).wait_send()
-            return carry
-
-        lax.fori_loop(1, NI, rs_sent, 0)
-    out_r.wait()
+            rs_copy(it, k, r_at).wait_send()
+            return carry
+
+        lax.fori_loop(1, NR, rs_sent, 0)
 
 
 def on_device(start_potentials, conductivity, electrodes, coarse_inverse):
-    shape = jax.ShapeDtypeStruct((B, B, B, F), F32)
+    shape = pltpu.VMEM((B, B, B, F), F32)
     tiles = lambda *lead: pltpu.VMEM(tuple(lead) + (2, 8, F), F32)
     dma = pltpu.SemaphoreType.DMA
     anywhere = pl.BlockSpec(memory_space=pl.ANY)
@@ -537,11 +559,10 @@
         kernel,
         out_shape=(shape, shape),
         in_specs=[anywhere, anywhere, pl.BlockSpec(memory_space=pltpu.VMEM), anywhere],
-        out_specs=(anywhere, anywhere),
+        out_specs=(pl.BlockSpec(memory_space=pltpu.VMEM),) * 2,
         scratch_shapes=[
             pltpu.VMEM((22, 32, 16), F32),
             pltpu.VMEM((16, 32), F32),
-            pltpu.VMEM((B, B, 16, F), F32),
             tiles(ITERS + 1, 22, 22),
             tiles(20, 20),
             tiles(22, 22),
@@ -552,24 +573,22 @@
             tiles(20, 20),
             tiles(20, 20),
             tiles(20, 20),
-            pltpu.VMEM((B, B, 16, F), F32),
-            pltpu.VMEM((256, 512), F32),
+            pltpu.VMEM((512, 256), F32),
             pltpu.VMEM((ITERS, BLK, F), F32),
-            pltpu.VMEM((ITERS, NQ, 2, BLK, F), F32),
             pltpu.VMEM((ITERS, 256, F), F32),
-            pltpu.VMEM((ITERS, NI, BLK, F), F32),
+            pltpu.VMEM((ITERS, 512, F), F32),
+            pltpu.VMEM((ITERS, NR, BLK, F), F32),
             pltpu.VMEM((128, F), F32),
             pltpu.VMEM((128, F), F32),
             dma((8,)), dma((8,)),
             dma((ITERS + 1, 16)), dma((ITERS + 1, 16)),
-            dma((NI,)), dma((NI,)),
-            dma((ITERS, NQ)), dma((ITERS, NQ)),
-            dma((ITERS,)), dma((ITERS,)),
-            dma((ITERS, NI)), dma((ITERS, NI)),
-            dma((3,)),
+            dma((2, NR)), dma((2, NR)),
+            dma((ITERS, NK)), dma((ITERS, NK)),
+            dma((ITERS, NR)), dma((ITERS, NR)),
+            dma((4,)),
         ],
         compiler_params=pltpu.CompilerParams(
-            collective_id=0, has_side_effects=True, vmem_limit_bytes=56 * 2**20
+            collective_id=0, has_side_effects=True, vmem_limit_bytes=50 * 2**20
         ),
         cost_estimate=pl.CostEstimate(flops=10**8, bytes_accessed=10**7, transcendentals=0),
     )(start_potentials, conductivity, electrodes.T, coarse_inverse)

time: 96.6 us -> 79.2 us (0.82)
  Pallas kernels: 91.3 us -> 75.5 us
  local copies, waits for them, and re-layouts: 4.57 us -> 2.64 us
    pallas_call x1, Pallas kernels: 91.3 us -> 75.5 us  [on_device(): pl.pallas_call(kernel, out_shape=(shape, shape), in_specs=[anywhere, anyw...]
    unnamed x4 -> x2, local copies, waits for them, and re-layouts: 4.57 us -> 2.64 us
where the time goes in v3:
time: 79.2 us; the launch traced here: 78.8 us
  Pallas kernels  75.5 us (95%)
  local copies, waits for them, and re-layouts  2.64 us (3%)
    pallas_call x1, Pallas kernels, on_device(): pl.pallas_call(kernel, out_shape=(shape, shape), in_specs=[anywhere, anyw...  75.5 us
    unnamed x2, local copies, waits for them, and re-layouts  2.64 us

profile of v3, /device:TPU:5, one launch (start us, length us, event | category | flops | bytes accessed | tf_op | source)
XLA Modules:
  0.0 78.8 jit_solution(15321126994160273030)
XLA Ops:
  0.6 75.5 %shard_map.59 = (f32[16,16,16,128]{3,2,1,0:T(8,128)S(1)}, f32[16,16,16,128]{3,2,1,0:T(8,128)S(1)}) custom-call(f32[16,16,16,128]{3,2,1,0:T(8,128)} %v_hbm.1, f32[16,16,16]{2,1,0:T(8,128)} %cond_ref.1, s32[2,128]{1,0:T(2,128)} %bitcast.1, f32[32,4096]{1,0:T(8,128)} %cinv_hbm.1), custom_call_target="tpu_custom_call" | custom-call | flops 100000000 | bytes 10000000 | tf_op jit(solution)/shard_map/pallas_call | solution.py:558
  76.1 1.3 %copy.8 = f32[16,16,16,128]{3,2,1,0:T(8,128)} copy(f32[16,16,16,128]{3,2,1,0:T(8,128)S(1)} %get-tuple-element.2) | data formatting | bytes 4194304
  77.5 1.3 %copy.9 = f32[16,16,16,128]{3,2,1,0:T(8,128)} copy(f32[16,16,16,128]{3,2,1,0:T(8,128)S(1)} %get-tuple-element.3) | data formatting | bytes 4194304

commit v4 on v3

--- a/solution.py
+++ b/solution.py
@@ -412,6 +412,7 @@
     for it in range(ITERS):
         region(residual(it), 3, 14, 3, 14, 7, 2)
         near(it, "here")
+        far_y(it, "start")
         residual_own_rim(it)
 
         def restrict(n, carry):
@@ -434,7 +435,6 @@
             return carry
 
         lax.fori_loop(1, NK, ag_start, 0)
-        far_y(it, "start")
 
         region(sweep(bb, 1, into_a), 3, 14, 3, 14, 7, 2)
         region(sweep(e_a, 0, into_b), 4, 12, 4, 12, 6, 3)

time: 79.2 us -> 86.1 us (1.087); the launches traced: 78.8 us -> 84.7 us
  Pallas kernels: 75.5 us -> 81.4 us
    pallas_call x1, Pallas kernels: 75.5 us -> 81.4 us  [on_device(): pl.pallas_call(kernel, out_shape=(shape, shape), in_specs=[anywhere, anyw...]
where the time goes in v4:
time: 86.1 us; the launch traced here: 84.7 us
  Pallas kernels  81.4 us (95%)
  local copies, waits for them, and re-layouts  2.64 us (3%)
    pallas_call x1, Pallas kernels, on_device(): pl.pallas_call(kernel, out_shape=(shape, shape), in_specs=[anywhere, anyw...  81.4 us
    unnamed x2, local copies, waits for them, and re-layouts  2.64 us

profile of v4, /device:TPU:5, one launch (start us, length us, event | category | flops | bytes accessed | tf_op | source)
XLA Modules:
  0.0 84.7 jit_solution(13046985508043352142)
XLA Ops:
  0.6 81.4 %shard_map.59 = (f32[16,16,16,128]{3,2,1,0:T(8,128)S(1)}, f32[16,16,16,128]{3,2,1,0:T(8,128)S(1)}) custom-call(f32[16,16,16,128]{3,2,1,0:T(8,128)} %v_hbm.1, f32[16,16,16]{2,1,0:T(8,128)} %cond_ref.1, s32[2,128]{1,0:T(2,128)} %bitcast.1, f32[32,4096]{1,0:T(8,128)} %cinv_hbm.1), custom_call_target="tpu_custom_call" | custom-call | flops 100000000 | bytes 10000000 | tf_op jit(solution)/shard_map/pallas_call | solution.py:558
  82.0 1.3 %copy.8 = f32[16,16,16,128]{3,2,1,0:T(8,128)} copy(f32[16,16,16,128]{3,2,1,0:T(8,128)S(1)} %get-tuple-element.2) | data formatting | bytes 4194304
  83.4 1.3 %copy.9 = f32[16,16,16,128]{3,2,1,0:T(8,128)} copy(f32[16,16,16,128]{3,2,1,0:T(8,128)S(1)} %get-tuple-element.3) | data formatting | bytes 4194304
